TPU v7x, 256 devices: a whole 4x4x8 slice. The times are simulated.
256 devices in a mesh: dp: 8 (over x, core), mp: 32 (over y, z).
Axes of the slice: x: 4, y: 4, z: 8, core: 2. Of those that a mesh axis runs over, the one named last changes fastest.
Arguments:
- hidden: bfloat16 [3072, 26624], P('dp', 'mp'), may hold values from -6 to 6
- down_weight: bfloat16 [26624, 8192], P('mp', 'dp'), may hold values from -0.0390625 to 0.0390625
- adapter_down: bfloat16 [32, 26624, 64], P('dp', 'mp'), may hold values from -0.0390625 to 0.0390625
- adapter_up: bfloat16 [32, 64, 8192], P('dp', None, 'mp'), may hold values from -0.1875 to 0.1875
- output_grad: bfloat16 [3072, 8192], P('dp', 'mp'), may hold values from -6 to 6
- adapter_per_block: int32 [24], replicated, may hold values from 0 to 31, as said below
- live_rows: int32 [8], replicated, may hold values from 96 to 384, as said below
Outputs:
- layer_out: bfloat16 [3072, 8192], P('dp', 'mp')
- hidden_gradient: bfloat16 [3072, 26624], P('dp', 'mp')
- down_grad: bfloat16 [32, 26624, 64], P('dp', 'mp')
- up_grad: bfloat16 [32, 64, 8192], P('dp', None, 'mp')
Inputs may be any that keep to these rules, and one draw needn't show every extreme that they name: `adapter_per_block`: adapter k is owned by index k // 4 of dp; the 3 blocks of one index of dp use adapters of 3 different owners. `live_rows`: some index of dp has all 384 rows live.
All inputs are finite; a program needn't handle non-finite values.
Results may differ from a plain program's by a relative error of at most 0.0055.
Values may be sent and summed in bfloat16 or wider, within the bound.
A program may use at most 128 MiB of HBM per device.

v0:
```python
import jax
import jax.numpy as jnp
from jax import lax
from jax.sharding import PartitionSpec as P

BLK = 128


def shards(
    hidden, down_weight, adapter_down, adapter_up, output_grad, adapter_per_block, live_rows
):
    dp_count = lax.axis_size("dp")
    dp_index = lax.axis_index("dp")
    row_count = hidden.shape[0]
    local_unit_index = hidden.shape[1]
    model_local = output_grad.shape[1]
    owned_count = adapter_down.shape[0]
    block_count = row_count // BLK
    id_table = adapter_per_block.reshape(dp_count, block_count)
    own_ids = lax.dynamic_slice_in_dim(id_table, dp_index, 1, 0)[0]
    own_owners = own_ids // owned_count
    live_count = lax.dynamic_slice_in_dim(live_rows, dp_index, 1, 0)[0]
    live_mask = (jnp.arange(row_count, dtype=jnp.int32) < live_count)[:, None]
    masked_grad = jnp.where(live_mask, output_grad, jnp.zeros_like(output_grad))
    source_ids = jnp.arange(dp_count, dtype=jnp.int32)
    local_ids = dp_index * owned_count + jnp.arange(owned_count, dtype=jnp.int32)
    wanted = jnp.sum(
        (id_table[:, :, None] == local_ids[None, None, :]).astype(jnp.int32), axis=1
    ).astype(jnp.bfloat16)
    every_down, every_up = (
        lax.all_gather(adapter_down, "dp", axis=0, tiled=True),
        lax.all_gather(adapter_up, "dp", axis=0, tiled=True),
    )
    all_ids = jnp.arange(owned_count * dp_count, dtype=jnp.int32)
    select = (own_ids[:, None] == all_ids[None, :]).astype(jnp.bfloat16)
    block_down = jnp.einsum(
        "bk,kfr->bfr", select, every_down, preferred_element_type=jnp.float32
    ).astype(jnp.bfloat16)
    block_up = jnp.einsum(
        "bk,krd->brd", select, every_up, preferred_element_type=jnp.float32
    ).astype(jnp.bfloat16)
    hid_blocks = hidden.reshape(block_count, BLK, local_unit_index)
    grad_blocks = masked_grad.reshape(block_count, BLK, model_local)
    down_part = jnp.einsum(
        "btf,bfr->btr", hid_blocks, block_down, preferred_element_type=jnp.float32
    )
    up_part = jnp.einsum("btd,brd->btr", grad_blocks, block_up, preferred_element_type=jnp.float32)
    down_sum, up_sum = lax.psum((down_part, up_part), "mp")
    down_act = down_sum.astype(jnp.bfloat16)
    up_act = up_sum.astype(jnp.bfloat16)
    grad_full = lax.all_gather(masked_grad, "mp", axis=1, tiled=True)
    panel = lax.all_gather(down_weight, "dp", axis=1, tiled=True)
    product = jnp.dot(hidden, panel, preferred_element_type=jnp.float32)
    partial_value = product
    back_sum = lax.dot_general(
        grad_full, panel, (((1,), (1,)), ((), ())), preferred_element_type=jnp.float32
    )
    partial_value, backward = (partial_value, back_sum)
    base_out = lax.psum_scatter(partial_value, "mp", scatter_dimension=1, tiled=True)
    branch = jnp.einsum(
        "btr,brd->btd", down_act, block_up, preferred_element_type=jnp.float32
    ).reshape(row_count, model_local)
    layer_out = jnp.where(live_mask, base_out + branch, jnp.float32(0.0)).astype(jnp.bfloat16)
    side_back = jnp.einsum(
        "btr,bfr->btf", up_act, block_down, preferred_element_type=jnp.float32
    ).reshape(row_count, local_unit_index)
    hidden_gradient = (backward + side_back).astype(jnp.bfloat16)
    term_down = jnp.einsum(
        "btf,btr->bfr", hid_blocks, up_act, preferred_element_type=jnp.float32
    ).astype(jnp.bfloat16)
    term_up = jnp.einsum(
        "btr,btd->brd", down_act, grad_blocks, preferred_element_type=jnp.float32
    ).astype(jnp.bfloat16)
    routing = (source_ids[:, None] == own_owners[None, :]).astype(jnp.bfloat16)
    back_down = jnp.einsum(
        "ob,bfr->ofr", routing, term_down, preferred_element_type=jnp.float32
    ).astype(jnp.bfloat16)
    back_up = jnp.einsum(
        "ob,brd->ord", routing, term_up, preferred_element_type=jnp.float32
    ).astype(jnp.bfloat16)
    arrived_down, arrived_up = (
        lax.all_to_all(back_down, "dp", split_axis=0, concat_axis=0, tiled=True),
        lax.all_to_all(back_up, "dp", split_axis=0, concat_axis=0, tiled=True),
    )
    down_grad = jnp.einsum(
        "sa,sfr->afr", wanted, arrived_down, preferred_element_type=jnp.float32
    ).astype(jnp.bfloat16)
    up_grad = jnp.einsum(
        "sa,srd->ard", wanted, arrived_up, preferred_element_type=jnp.float32
    ).astype(jnp.bfloat16)
    return (layer_out, hidden_gradient, down_grad, up_grad)


def solution(mesh):
    return jax.shard_map(
        shards,
        mesh=mesh,
        in_specs=(
            P("dp", "mp"),
            P("mp", "dp"),
            P("dp", "mp", None),
            P("dp", None, "mp"),
            P("dp", "mp"),
            P(),
            P(),
        ),
        out_specs=(P("dp", "mp"), P("dp", "mp"), P("dp", "mp", None), P("dp", None, "mp")),
        check_vma=False,
    )
```

profile of v0, /device:TPU:1, one launch (start us, length us, event | category | flops | bytes accessed | tf_op | source)
XLA Modules:
  0.0 493.1 jit_solution(3603705888861838775)
XLA Ops:
  7.2 0.7 all-gather.5.cloned.1.call-update
  7.9 0.7 all-gather.9.cloned.1.call-update
  8.7 0.7 all-gather.7.cloned.1.call-update
  9.4 1.2 dynamic_slice.6
  11.3 1.7 broadcast_select_fusion
  13.1 75.2 %all-gather.5.cloned.1.call-done = bf16[832,8192]{1,0:T(8,128)(2,1)} async-done(((bf16[832,1024]{1,0:T(8,128)(2,1)}), bf16[832,8192]{1,0:T(8,128)(2,1)}) %all-gather.5.cloned.1.call-update) | async-done | bytes 13631504 | tf_op jit(solution)/shard_map/all_gather | solution.py:52
  88.3 12.6 %fusion.35 = f32[384,8192]{1,0:T(8,128)} fusion(bf16[384,832]{0,1:T(8,128)(2,1)} %param.7, bf16[832,8192]{1,0:T(8,128)(2,1)} %all-gather.5.cloned.1.call-done), kind=kOutput, calls=%fused_computation.53 | convolution fusion | flops 5234491392 | bytes 26853376 | tf_op jit(solution)/shard_map/dot_general | solution.py:53
  101.0 1.1 copy-done.1
  102.6 14.0 %all-gather.9.cloned.1.call-done = bf16[32,64,256]{2,1,0:T(8,128)(2,1)} async-done(((bf16[4,64,256]{2,1,0:T(8,128)(2,1)}), bf16[32,64,256]{2,1,0:T(8,128)(2,1)}) %all-gather.9.cloned.1.call-update) | async-done | bytes 1048592 | tf_op jit(solution)/shard_map/all_gather | solution.py:32
  116.6 1.9 fusion.4
  118.7 32.1 %all-gather.7.cloned.1.call-done = bf16[32,832,64]{1,2,0:T(8,128)(2,1)} async-done(((bf16[4,832,64]{1,2,0:T(8,128)(2,1)}), bf16[32,832,64]{1,2,0:T(8,128)(2,1)}) %all-gather.7.cloned.1.call-update) | async-done | bytes 3407888 | tf_op jit(solution)/shard_map/all_gather | solution.py:31
  150.9 5.0 %fusion = bf16[3,832,64]{1,0,2:T(4,128)(2,1)S(1)} fusion(bf16[32,832,64]{1,2,0:T(8,128)(2,1)} %all-gather.7.cloned.1.call-done, s32[3]{0:T(128)S(1)} %get-tuple-element.27), kind=kOutput, calls=%fused_computation | convolution fusion | flops 10223712 | bytes 3727372 | tf_op jit(solution)/shard_map/bk,kfr->bfr/dot_general | solution.py:36
  156.2 118.2 %all-reduce.2 = (bf16[3,128,64]{1,2,0:T(8,128)(2,1)S(1)}, bf16[3,128,64]{1,2,0:T(8,128)(2,1)S(1)}) all-reduce(f32[3,128,64]{1,2,0:T(8,128)S(1)} %convolution_bitcast_fusion, f32[3,128,64]{1,2,0:T(8,128)S(1)} %fusion.18), channel_id=1, replica_groups=mesh['dp'=8,'mp'=32] {'mp'}, use_global_device_ids=true, to_apply=%region_1.2 | all-reduce | flops 49152 | bytes 294912 | tf_op jit(solution)/shard_map/psum | solution.py:48
  274.9 0.8 copy.86
  275.7 31.1 %all-to-all-start.1 = ((bf16[8,64,256]{2,1,0:T(8,128)(2,1)}), bf16[8,64,256]{2,1,0:T(8,128)(2,1)S(1)}, u32[]{:S(2)}, u32[]{:S(2)}) async-start(bf16[8,64,256]{2,1,0:T(8,128)(2,1)} %copy.86), calls=%async_computation.2 | async-start | bytes 524288 | tf_op jit(solution)/shard_map/all_to_all | solution.py:83
  307.6 1.1 copy.83
  308.7 4.6 all-to-all-done.1
  313.3 4.5 all-to-all-start
  318.3 1.5 copy.79
  321.0 10.6 %all-to-all-done = bf16[8,832,64]{1,2,0:T(8,128)(2,1)S(1)} async-done(((bf16[8,832,64]{1,2,0:T(8,128)(2,1)}), bf16[8,832,64]{1,2,0:T(8,128)(2,1)S(1)}, u32[]{:S(2)}, u32[]{:S(2)}) %all-to-all-start) | async-done | bytes 852000 | tf_op jit(solution)/shard_map/all_to_all | solution.py:82
  332.2 0.8 copy.88
  333.0 13.5 %fusion.2 = bf16[384,832]{0,1:T(8,128)(2,1)} fusion(f32[384,832]{0,1:T(8,128)} %copy.79, bf16[384,8192]{1,0:T(8,128)(2,1)} %all-gather.11.cloned.1.call-done, bf16[832,8192]{1,0:T(8,128)(2,1)} %all-gather.5.cloned.1.call-done), kind=kOutput, calls=%fused_computation.4 | convolution fusion | flops 5235130368 | bytes 21839872 | tf_op jit(solution)/shard_map/dot_general | solution.py:55
  346.5 138.3 %reduce-scatter.2.cloned.1.call-done = f32[384,256]{1,0:T(8,128)} async-done(((f32[384,8192]{1,0:T(8,128)}), f32[384,256]{1,0:T(8,128)}) %reduce-scatter.2.cloned.1.call-update) | async-done | bytes 393232 | tf_op jit(solution)/shard_map/reduce_scatter | solution.py:59
  484.8 1.8 fusion.9
  (31 shorter events, 5.6 us)
Async XLA Ops:
  7.2 81.2 %all-gather.5.cloned.1.call-start = ((), (), s32[]{:S(2)}) async-start(), calls=%async_computation.3 | async-start | bytes 15335424 | tf_op jit(solution)/shard_map/all_gather | solution.py:52
  7.9 108.7 %all-gather.9.cloned.1.call-start = ((), (), s32[]{:S(2)}) async-start(), calls=%async_computation.6 | async-start | bytes 1179648 | tf_op jit(solution)/shard_map/all_gather | solution.py:32
  8.6 142.2 %all-gather.7.cloned.1.call-start = ((), (), s32[]{:S(2)}) async-start(), calls=%async_computation.5 | async-start | bytes 4128768 | tf_op jit(solution)/shard_map/all_gather | solution.py:31
  9.4 323.6 %all-gather.11.cloned.1.call-start = ((), (), s32[]{:S(2)}) async-start(), calls=%async_computation.7 | async-start | bytes 6488064 | tf_op jit(solution)/shard_map/all_gather | solution.py:51
  13.1 471.7 %reduce-scatter.2.cloned.1.call-start = ((), (), s32[]{:S(2)}) async-start(), calls=%async_computation.4 | async-start | bytes 12976128 | tf_op jit(solution)/shard_map/reduce_scatter | solution.py:59
  101.0 1.1 copy-start.1
  101.0 1.4 copy-start.2
  101.0 17.5 %copy-start = (bf16[384,256]{1,0:T(8,128)(2,1)S(1)}, bf16[384,256]{1,0:T(8,128)(2,1)}, u32[]{:S(2)}) copy-start(bf16[384,256]{1,0:T(8,128)(2,1)} %broadcast_select_fusion) | copy-start | bytes 589828
  275.7 37.6 %all-to-all-start.1 = ((bf16[8,64,256]{2,1,0:T(8,128)(2,1)}), bf16[8,64,256]{2,1,0:T(8,128)(2,1)S(1)}, u32[]{:S(2)}, u32[]{:S(2)}) async-start(bf16[8,64,256]{2,1,0:T(8,128)(2,1)} %copy.86), calls=%async_computation.2 | async-start | bytes 524288 | tf_op jit(solution)/shard_map/all_to_all | solution.py:83
  313.3 18.2 %all-to-all-start = ((bf16[8,832,64]{1,2,0:T(8,128)(2,1)}), bf16[8,832,64]{1,2,0:T(8,128)(2,1)S(1)}, u32[]{:S(2)}, u32[]{:S(2)}) async-start(bf16[8,832,64]{1,2,0:T(8,128)(2,1)} %copy.83), calls=%async_computation.1 | async-start | bytes 1835008 | tf_op jit(solution)/shard_map/all_to_all | solution.py:82
Sparse Core Ops, SparseCore 0:
  9.8 78.4 all-gather.4
  90.2 26.3 all-gather.8
  118.5 32.3 all-gather.6
  153.7 90.5 all-gather.10
  248.3 236.3 reduce-scatter.1
where the time goes:
time: 497 us; the launch traced here: 493 us
  waiting for transfers between devices  277 us (56%)
  blocking collectives  118 us (24%)
  matrix products  36.4 us (7%)
  starting transfers between devices  35.8 us (7%)
  between operations  13.9 us (3%)
  local copies, waits for them, and re-layouts  7.66 us (2%)
    reduce_scatter x1, waiting for transfers between devices, shards(): lax.psum_scatter(partial_value, 'mp', scatter_dimension=1, tiled=True)  138 us
    psum x1, blocking collectives, shards(): down_sum, up_sum = lax.psum((down_part, up_part), 'mp')  118 us
    all_gather x1, waiting for transfers between devices, shards(): panel = lax.all_gather(down_weight, 'dp', axis=1, tiled=True)  75.2 us
    all_gather x1, waiting for transfers between devices, shards(): lax.all_gather(adapter_down, 'dp', axis=0, tiled=True)  32.1 us
    all_to_all x1, starting transfers between devices, shards(): lax.all_to_all(back_up, 'dp', split_axis=0, concat_axis=0, tiled=True)  31.1 us
    all_gather x1, waiting for transfers between devices, shards(): lax.all_gather(adapter_up, 'dp', axis=0, tiled=True)  14 us
    dot_general x1, matrix products, shards(): lax.dot_general(grad_full, panel, (((1,), (1,)), ((), ())), preferred_ele...  13.5 us
    dot_general x1, matrix products, shards(): product = jnp.dot(hidden, panel, preferred_element_type=jnp.float32)  12.6 us
  transfers between devices with their start and end apart: 7, of which 6 were waited for; matrix products, arithmetic and copies ran while one was open for 9% of the time, Pallas kernels for 0%

commit v1 on v0

v1 whole, which is shorter than its diff:
```python
import jax
import jax.numpy as jnp
from jax import lax
from jax.experimental import pallas as pl
from jax.experimental.pallas import tpu as pltpu
from jax.sharding import PartitionSpec as P

BLK = 128
MESH = pl.DeviceIdType.MESH
f32, bf16 = jnp.float32, jnp.bfloat16


def rem(a, n):
    return lax.rem(a, n)


def kernel(live_ref, hid, w_hbm, grad, branch, side, out, dh,
           Wp, Gg, Zs, Zr, Ys, Yr, Sown, acc, dacc,
           lS, wS, wR, gS, gR, zS, zR, yS, yR):
    dp, mp = lax.axis_index("dp"), lax.axis_index("mp")
    x, c, y, z = dp // 2, rem(dp, 2), mp // 8, rem(mp, 8)

    def dev(dx=0, dc=0, dy=0, dz=0):
        return (rem(x + dx, 4) * 2 + rem(c + dc, 2), rem(y + dy, 4) * 8 + rem(z + dz, 8))

    XP, XM, SIB = dev(dx=1), dev(dx=3), dev(dc=1)
    YP, YM, Y2, ZP, ZM = dev(dy=1), dev(dy=3), dev(dy=2), dev(dz=1), dev(dz=7)

    bar = pltpu.get_barrier_semaphore()
    peers = (XP, XM, SIB, YP, YM, Y2, ZP, ZM)
    for p in peers:
        pl.semaphore_signal(bar, inc=1, device_id=p, device_id_type=MESH)

    wbase = x * 8 + c * 4
    loc = [pltpu.make_async_copy(w_hbm.at[:, pl.ds(256 * i, 256)], Wp.at[wbase + i], lS.at[i]) for i in range(4)]
    for cp in loc:
        cp.start()
    gslot = y * 8 + z
    gl = pltpu.make_async_copy(grad, Gg.at[gslot], lS.at[4])
    gl.start()
    pl.semaphore_wait(bar, len(peers))

    sends = []

    def put(src, dst, ss, rs, to):
        cp = pltpu.make_async_remote_copy(src_ref=src, dst_ref=dst, send_sem=ss, recv_sem=rs, device_id=to, device_id_type=MESH)
        cp.start()
        sends.append(cp)

    def got(dst, ss, rs):
        pltpu.make_async_remote_copy(src_ref=dst, dst_ref=dst, send_sem=ss, recv_sem=rs, device_id=XP, device_id_type=MESH).wait_recv()

    def wsl(dx, i, n, dc=0):
        return Wp.at[pl.ds(rem(x + dx, 4) * 8 + rem(c + dc, 2) * 4 + i, n)]

    def wput(k, dx, i, n, to):
        put(wsl(dx, i, n), wsl(dx, i, n), wS.at[k], wR.at[k], to)

    def wgot(k, dx, i, n, dc=0):
        got(wsl(dx, i, n, dc), wS.at[k], wR.at[k])

    def gsl(dy, j, n):
        return Gg.at[pl.ds(rem(y + dy, 4) * 8 + j, n)]

    def gz(dz, lo=0, n=384):
        return Gg.at[y * 8 + rem(z + dz, 8), pl.ds(lo, n)]

    def gput(k, ref, to):
        put(ref, ref, gS.at[k], gR.at[k], to)

    gl.wait()
    gput(0, gz(0), ZP)
    gput(1, gz(0), ZM)
    for cp in loc:
        cp.wait()
    wput(0, 0, 0, 2, XP)
    wput(2, 0, 2, 2, XM)
    wput(6, 0, 0, 4, SIB)
    wput(1, 0, 2, 2, XP)
    wput(3, 0, 0, 2, XM)

    def product(yt, zt):
        acc[...] = jnp.dot(hid[...], Wp[yt * 8 + zt], preferred_element_type=f32)

    def zcopy(r, slot, h, to):
        s = pltpu.make_async_remote_copy(
            src_ref=Zs.at[r, slot, h], dst_ref=Zr.at[r, slot, h], send_sem=zS.at[r, slot, h],
            recv_sem=zR.at[r, slot, h], device_id=to, device_id_type=MESH)
        return s

    def half(h):
        return acc[pl.ds(192 * h, 192)]

    def level0(r, yt):
        product(yt, rem(z + 4, 8))
        for h, to in ((0, ZM), (1, ZP)):
            Zs[r, 0, h] = half(h).astype(bf16)
            zcopy(r, 0, h, to).start()

    def level1(r, yt):
        for s, to in ((0, ZM), (1, ZP)):
            product(yt, rem(z + (5 if s == 0 else 3), 8))
            slot = 1 + s
            Zs[r, slot, 1 - s] = half(1 - s).astype(bf16)
            zcopy(r, slot, 1 - s, to).start()
            zcopy(r, 0, s, to).wait_recv()
            Zs[r, slot, s] = (half(s) + Zr[r, 0, s].astype(f32)).astype(bf16)
            zcopy(r, slot, s, to).start()

    def level23(r, yt, l):
        for s, to in ((0, ZM), (1, ZP)):
            product(yt, rem(z + (4 + l if s == 0 else 4 - l), 8))
            slot = 2 * l - 1 + s
            for h in (1 - s, s):
                zcopy(r, slot - 2, h, to).wait_recv()
                Zs[r, slot, h] = (half(h) + Zr[r, slot - 2, h].astype(f32)).astype(bf16)
                zcopy(r, slot, h, to).start()

    def ycopy(r, yt):
        j = rem(y - yt + 4, 4)
        return pltpu.make_async_remote_copy(
            src_ref=Ys.at[r], dst_ref=Yr.at[j - 1], send_sem=yS.at[r], recv_sem=yR.at[j - 1],
            device_id=(dp, yt * 8 + z), device_id_type=MESH)

    def level4(r, yt):
        product(yt, z)
        for h in (0, 1):
            for slot in (5, 6):
                zcopy(r, slot, h, ZP).wait_recv()
            acc[pl.ds(192 * h, 192)] = half(h) + (Zr[r, 5, h].astype(f32) + Zr[r, 6, h].astype(f32))

        @pl.when(y == yt)
        def _():
            Sown[...] = acc[...]

        @pl.when(y != yt)
        def _():
            Ys[r] = acc[...].astype(bf16)
            ycopy(r, yt).start()

    def back(m, n=2):
        g = jnp.concatenate([Gg[m + i] for i in range(n)], axis=1)
        w = jnp.concatenate([Wp[m + i] for i in range(n)], axis=1)
        dacc[...] += lax.dot_general(g, w, (((1,), (1,)), ((), ())), preferred_element_type=f32)

    def backs(yt):
        def b(i, _):
            back(yt * 8 + 2 * i)
            return 0
        lax.fori_loop(0, 4, b, 0)

    dacc[...] = side[...]
    y0, y1, y2, y3 = x, rem(x + 3, 4), rem(x + 1, 4), rem(x + 2, 4)

    wgot(6, 0, 0, 4, 1)
    level0(0, y0)
    got(gz(7), gS.at[0], gR.at[0]); gput(2, gz(7), ZP)
    got(gz(1), gS.at[1], gR.at[1]); gput(3, gz(1), ZM)
    level1(0, y0)
    got(gz(6), gS.at[2], gR.at[2]); gput(4, gz(6), ZP)
    got(gz(2), gS.at[3], gR.at[3]); gput(5, gz(2), ZM)
    level23(0, y0, 2)
    got(gz(5), gS.at[4], gR.at[4]); gput(6, gz(5, 0, 192), ZP)
    got(gz(3), gS.at[5], gR.at[5]); gput(7, gz(3, 192, 192), ZM)
    level23(0, y0, 3)
    got(gz(4, 0, 192), gS.at[6], gR.at[6])
    got(gz(4, 192, 192), gS.at[7], gR.at[7])
    gput(8, gsl(0, 0, 4), YP)
    gput(10, gsl(0, 4, 4), YM)
    gput(9, gsl(0, 4, 4), YP)
    gput(11, gsl(0, 0, 4), YM)
    level4(0, y0)

    wgot(0, 3, 0, 2); wput(4, 3, 0, 2, XP); wput(7, 3, 0, 2, SIB)
    wgot(2, 1, 2, 2); wput(5, 1, 2, 2, XM); wput(9, 1, 2, 2, SIB)
    wgot(1, 3, 2, 2); wput(8, 3, 2, 2, SIB)
    wgot(3, 1, 0, 2); wput(10, 1, 0, 2, SIB)
    wgot(7, 3, 0, 2, 1); wgot(8, 3, 2, 2, 1); wgot(9, 1, 2, 2, 1); wgot(10, 1, 0, 2, 1)

    def both(fn, *a):
        def b(i, _):
            fn(1 + i, rem(x + 3 - 2 * i, 4), *a)
            return 0
        lax.fori_loop(0, 2, b, 0)

    both(level0)
    both(level1)
    both(level23, 2)
    got(gsl(3, 0, 4), gS.at[8], gR.at[8]); gput(12, gsl(3, 0, 4), YP)
    got(gsl(1, 4, 4), gS.at[10], gR.at[10]); gput(13, gsl(1, 4, 4), YM)
    both(level23, 3)
    both(level4)

    wgot(4, 2, 0, 2); wput(11, 2, 0, 2, SIB)
    wgot(5, 2, 2, 2); wput(12, 2, 2, 2, SIB)
    wgot(11, 2, 0, 2, 1); wgot(12, 2, 2, 2, 1)
    level0(3, y3)
    got(gsl(3, 4, 4), gS.at[9], gR.at[9])
    got(gsl(1, 0, 4), gS.at[11], gR.at[11])
    got(gsl(2, 0, 4), gS.at[12], gR.at[12])
    got(gsl(2, 4, 4), gS.at[13], gR.at[13])
    level1(3, y3)
    backs(y0)
    level23(3, y3, 2)
    backs(y1)
    level23(3, y3, 3)
    backs(y2)
    level4(3, y3)
    backs(y3)

    live = live_ref[0]
    rows = lax.broadcasted_iota(jnp.int32, (384, 1), 0)
    dh[...] = jnp.where(rows < live, dacc[...], 0.0).astype(bf16)
    for j in range(3):
        pltpu.make_async_remote_copy(src_ref=Yr.at[j], dst_ref=Yr.at[j], send_sem=yS.at[0], recv_sem=yR.at[j], device_id=XP, device_id_type=MESH).wait_recv()
    total = (Sown[...] + branch[...]) + (Yr[0].astype(f32) + Yr[1].astype(f32) + Yr[2].astype(f32))
    out[...] = jnp.where(rows < live, total, 0.0).astype(bf16)

    for cp in sends:
        cp.wait_send()

    def zw(i, _):
        r, slot = i // 7, rem(i, 7)
        for h in (0, 1):
            zcopy(r, slot, h, ZP).wait_send()
        return 0
    lax.fori_loop(0, 28, zw, 0)
    for r, yt in enumerate((y0, y1, y2, y3)):
        @pl.when(y != yt)
        def _():
            ycopy(r, yt).wait_send()


def core_call(live, hid, w, grad, branch, side):
    V = pl.BlockSpec(memory_space=pltpu.VMEM)
    D = pltpu.SemaphoreType.DMA
    return pl.pallas_call(
        kernel,
        out_shape=(jax.ShapeDtypeStruct((384, 256), bf16), jax.ShapeDtypeStruct((384, 832), bf16)),
        in_specs=[pl.BlockSpec(memory_space=pltpu.SMEM), V, pl.BlockSpec(memory_space=pl.ANY), V, V, V],
        out_specs=(V, V),
        scratch_shapes=[
            pltpu.VMEM((32, 832, 256), bf16),
            pltpu.VMEM((32, 384, 256), bf16),
            pltpu.VMEM((4, 7, 2, 192, 256), bf16),
            pltpu.VMEM((4, 7, 2, 192, 256), bf16),
            pltpu.VMEM((4, 384, 256), bf16),
            pltpu.VMEM((3, 384, 256), bf16),
            pltpu.VMEM((384, 256), f32),
            pltpu.VMEM((384, 256), f32),
            pltpu.VMEM((384, 832), f32),
            D((5,)), D((13,)), D((13,)), D((14,)), D((14,)),
            D((4, 7, 2)), D((4, 7, 2)), D((4,)), D((3,)),
        ],
        name="base_layer",
        cost_estimate=pl.CostEstimate(flops=2 * 2 * 384 * 832 * 8192, bytes_accessed=6 * 2 ** 20, transcendentals=0),
        compiler_params=pltpu.CompilerParams(collective_id=0, has_side_effects=True, vmem_limit_bytes=58 * 2 ** 20),
    )(live, hid, w, grad, branch, side)


def shards(hidden, down_weight, adapter_down, adapter_up, output_grad, adapter_per_block, live_rows):
    dp_count = lax.axis_size("dp")
    dp_index = lax.axis_index("dp")
    row_count = hidden.shape[0]
    local_unit_index = hidden.shape[1]
    model_local = output_grad.shape[1]
    owned_count = adapter_down.shape[0]
    block_count = row_count // BLK
    id_table = adapter_per_block.reshape(dp_count, block_count)
    own_ids = lax.dynamic_slice_in_dim(id_table, dp_index, 1, 0)[0]
    own_owners = own_ids // owned_count
    live_count = lax.dynamic_slice_in_dim(live_rows, dp_index, 1, 0)
    live_mask = (jnp.arange(row_count, dtype=jnp.int32) < live_count[0])[:, None]
    masked_grad = jnp.where(live_mask, output_grad, jnp.zeros_like(output_grad))
    source_ids = jnp.arange(dp_count, dtype=jnp.int32)
    local_ids = dp_index * owned_count + jnp.arange(owned_count, dtype=jnp.int32)
    wanted = jnp.sum((id_table[:, :, None] == local_ids[None, None, :]).astype(jnp.int32), axis=1).astype(jnp.bfloat16)
    every_down, every_up = (lax.all_gather(adapter_down, "dp", axis=0, tiled=True), lax.all_gather(adapter_up, "dp", axis=0, tiled=True))
    all_ids = jnp.arange(owned_count * dp_count, dtype=jnp.int32)
    select = (own_ids[:, None] == all_ids[None, :]).astype(jnp.bfloat16)
    block_down = jnp.einsum("bk,kfr->bfr", select, every_down, preferred_element_type=jnp.float32).astype(jnp.bfloat16)
    block_up = jnp.einsum("bk,krd->brd", select, every_up, preferred_element_type=jnp.float32).astype(jnp.bfloat16)
    hid_blocks = hidden.reshape(block_count, BLK, local_unit_index)
    grad_blocks = masked_grad.reshape(block_count, BLK, model_local)
    down_part = jnp.einsum("btf,bfr->btr", hid_blocks, block_down, preferred_element_type=jnp.float32)
    up_part = jnp.einsum("btd,brd->btr", grad_blocks, block_up, preferred_element_type=jnp.float32)
    down_sum, up_sum = lax.psum((down_part, up_part), "mp")
    down_act = down_sum.astype(jnp.bfloat16)
    up_act = up_sum.astype(jnp.bfloat16)
    branch = jnp.einsum("btr,brd->btd", down_act, block_up, preferred_element_type=jnp.float32).reshape(row_count, model_local)
    side_back = jnp.einsum("btr,bfr->btf", up_act, block_down, preferred_element_type=jnp.float32).reshape(row_count, local_unit_index)
    layer_out, hidden_gradient = core_call(live_count, hidden, down_weight, output_grad, branch, side_back)
    term_down = jnp.einsum("btf,btr->bfr", hid_blocks, up_act, preferred_element_type=jnp.float32).astype(jnp.bfloat16)
    term_up = jnp.einsum("btr,btd->brd", down_act, grad_blocks, preferred_element_type=jnp.float32).astype(jnp.bfloat16)
    routing = (source_ids[:, None] == own_owners[None, :]).astype(jnp.bfloat16)
    back_down = jnp.einsum("ob,bfr->ofr", routing, term_down, preferred_element_type=jnp.float32).astype(jnp.bfloat16)
    back_up = jnp.einsum("ob,brd->ord", routing, term_up, preferred_element_type=jnp.float32).astype(jnp.bfloat16)
    arrived_down, arrived_up = (
        lax.all_to_all(back_down, "dp", split_axis=0, concat_axis=0, tiled=True),
        lax.all_to_all(back_up, "dp", split_axis=0, concat_axis=0, tiled=True),
    )
    down_grad = jnp.einsum("sa,sfr->afr", wanted, arrived_down, preferred_element_type=jnp.float32).astype(jnp.bfloat16)
    up_grad = jnp.einsum("sa,srd->ard", wanted, arrived_up, preferred_element_type=jnp.float32).astype(jnp.bfloat16)
    return (layer_out, hidden_gradient, down_grad, up_grad)


def solution(mesh):
    return jax.shard_map(
        shards,
        mesh=mesh,
        in_specs=(P("dp", "mp"), P("mp", "dp"), P("dp", "mp", None), P("dp", None, "mp"), P("dp", "mp"), P(), P()),
        out_specs=(P("dp", "mp"), P("dp", "mp"), P("dp", "mp", None), P("dp", None, "mp")),
        check_vma=False,
    )
```

time: 497 us -> 374 us (0.75)
  waiting for transfers between devices: 277 us -> 63.4 us
  Pallas kernels: 0 us -> 117 us
  matrix products: 36.4 us -> 12.1 us
    reduce_scatter x1 -> x0, waiting for transfers between devices: 138 us -> none  [shards(): lax.psum_scatter(partial_value, 'mp', scatter_dimension=1, tiled=True)]
    pallas_call x0 -> x1, Pallas kernels: none -> 117 us  [core_call(): pl.pallas_call(kernel, out_shape=(jax.ShapeDtypeStruct((384, 256), bf16),...]
    all_gather x2 -> x0, waiting for transfers between devices: 75.2 us -> none  [the longest x1 75.2 us: shards(): panel = lax.all_gather(down_weight, 'dp', axis=1, tiled=True)]
    dot_general x2 -> x0, matrix products: 26.1 us -> none  [the longest x1 13.5 us: shards(): lax.dot_general(grad_full, panel, (((1,), (1,)), ((), ())), preferred_ele...]
    all_gather x1, waiting for transfers between devices: 14 us -> 26 us  [shards(): lax.all_gather(adapter_up, 'dp', axis=0, tiled=True)]
    all_to_all x1, waiting for transfers between devices: 10.6 us -> 0.01 us  [shards(): lax.all_to_all(back_down, 'dp', split_axis=0, concat_axis=0, tiled=True)]
  transfers between devices with their start and end apart: 7 -> 4, of which waited for: 6 -> 3; matrix products, arithmetic and copies ran while one was open for 9% -> 4% of each run, Pallas kernels for 0% -> 31%
where the time goes in v1:
time: 374 us; the launch traced here: 371 us
  blocking collectives  117 us (31%)
  Pallas kernels  117 us (31%)
  waiting for transfers between devices  63.4 us (17%)
  starting transfers between devices  35.8 us (10%)
  between operations  14.1 us (4%)
  matrix products  12.1 us (3%)
  local copies, waits for them, and re-layouts  9.74 us (3%)
    psum x1, blocking collectives, shards(): down_sum, up_sum = lax.psum((down_part, up_part), 'mp')  117 us
    pallas_call x1, Pallas kernels, core_call(): pl.pallas_call(kernel, out_shape=(jax.ShapeDtypeStruct((384, 256), bf16),...  117 us
    all_gather x1, waiting for transfers between devices, shards(): lax.all_gather(adapter_down, 'dp', axis=0, tiled=True)  32.1 us
    all_to_all x1, starting transfers between devices, shards(): lax.all_to_all(back_up, 'dp', split_axis=0, concat_axis=0, tiled=True)  31.2 us
    all_gather x1, waiting for transfers between devices, shards(): lax.all_gather(adapter_up, 'dp', axis=0, tiled=True)  26 us
  transfers between devices with their start and end apart: 4, of which 3 were waited for; matrix products, arithmetic and copies ran while one was open for 4% of the time, Pallas kernels for 31%

profile of v1, /device:TPU:1, one launch (start us, length us, event | category | flops | bytes accessed | tf_op | source)
XLA Modules:
  0.0 370.7 jit_solution(13199679695796181002)
XLA Ops:
  7.2 0.7 all-gather.5.cloned.1.call-update
  7.9 0.7 all-gather.3.cloned.1.call-update
  8.7 0.7 reshape.33
  9.4 1.4 copy.84.hid
  10.9 1.3 dynamic_slice.6.live_ref
  13.0 1.0 broadcast_select_fusion
  14.0 26.0 %all-gather.5.cloned.1.call-done = bf16[32,64,256]{2,1,0:T(8,128)(2,1)} async-done(((bf16[4,64,256]{2,1,0:T(8,128)(2,1)}), bf16[32,64,256]{2,1,0:T(8,128)(2,1)}) %all-gather.5.cloned.1.call-update) | async-done | bytes 1048592 | tf_op jit(solution)/shard_map/all_gather | solution.py:278
  40.0 1.9 fusion.3
  42.1 32.1 %all-gather.3.cloned.1.call-done = bf16[32,832,64]{1,2,0:T(8,128)(2,1)} async-done(((bf16[4,832,64]{1,2,0:T(8,128)(2,1)}), bf16[32,832,64]{1,2,0:T(8,128)(2,1)}) %all-gather.3.cloned.1.call-update) | async-done | bytes 3407888 | tf_op jit(solution)/shard_map/all_gather | solution.py:278
  74.2 5.0 %fusion = bf16[3,832,64]{1,0,2:T(4,128)(2,1)S(1)} fusion(bf16[32,832,64]{1,2,0:T(8,128)(2,1)} %all-gather.3.cloned.1.call-done, s32[3]{0:T(128)S(1)} %get-tuple-element.31), kind=kOutput, calls=%fused_computation | convolution fusion | flops 10223712 | bytes 3727372 | tf_op jit(solution)/shard_map/bk,kfr->bfr/dot_general | solution.py:281
  79.6 117.0 %all-reduce.2 = (bf16[3,128,64]{1,2,0:T(8,128)(2,1)S(1)}, bf16[3,128,64]{1,2,0:T(8,128)(2,1)S(1)}) all-reduce(f32[3,128,64]{1,2,0:T(8,128)S(1)} %convolution_bitcast_fusion, f32[3,128,64]{1,2,0:T(8,128)S(1)} %fusion.15), channel_id=1, replica_groups=mesh['dp'=8,'mp'=32] {'mp'}, use_global_device_ids=true, to_apply=%region_0.1 | all-reduce | flops 49152 | bytes 294912 | tf_op jit(solution)/shard_map/psum | solution.py:287
  196.6 1.5 fusion.10
  198.9 0.8 copy.91
  199.6 31.2 %all-to-all-start.1 = ((bf16[8,64,256]{2,1,0:T(8,128)(2,1)}), bf16[8,64,256]{2,1,0:T(8,128)(2,1)S(1)}, u32[]{:S(2)}, u32[]{:S(2)}) async-start(bf16[8,64,256]{2,1,0:T(8,128)(2,1)} %copy.91), calls=%async_computation.1 | async-start | bytes 524288 | tf_op jit(solution)/shard_map/all_to_all | solution.py:300
  231.4 1.1 copy.88
  232.5 1.0 fusion.13
  233.5 3.9 %all-to-all-done.1 = bf16[8,64,256]{2,1,0:T(8,128)(2,1)S(1)} async-done(((bf16[8,64,256]{2,1,0:T(8,128)(2,1)}), bf16[8,64,256]{2,1,0:T(8,128)(2,1)S(1)}, u32[]{:S(2)}, u32[]{:S(2)}) %all-to-all-start.1) | async-done | bytes 262176 | tf_op jit(solution)/shard_map/all_to_all | solution.py:300
  237.4 4.5 %all-to-all-start = ((bf16[8,832,64]{1,2,0:T(8,128)(2,1)}), bf16[8,832,64]{1,2,0:T(8,128)(2,1)S(1)}, u32[]{:S(2)}, u32[]{:S(2)}) async-start(bf16[8,832,64]{1,2,0:T(8,128)(2,1)} %copy.88), calls=%async_computation | async-start | bytes 1835008 | tf_op jit(solution)/shard_map/all_to_all | solution.py:299
  241.9 116.6 %base_layer.1 = (bf16[384,256]{1,0:T(8,128)(2,1)}, bf16[384,832]{1,0:T(8,128)(2,1)}) custom-call(s32[1]{0:T(128)} %dynamic_slice.6.live_ref, bf16[384,832]{1,0:T(8,128)(2,1)} %copy-done, bf16[832,1024]{1,0:T(8,128)(2,1)} %w_hbm.1, bf16[384,256]{1,0:T(8,128)(2,1)} %grad.1, f32[384,256]{1,0:T(8,128)} %bitcast.39, f32[384,832]{1,0:T(8,128)} %bitcast.38), custom_call_target="tpu_custom_call" | custom-call | flops 10468982784 | bytes 6291456 | tf_op jit(solution)/shard_map/base_layer/pallas_call | solution.py:237
  358.5 2.2 copy.93
  361.0 0.7 copy.95
  361.7 0.7 convolution_convert_fusion.1
  362.3 0.8 copy.94
  363.2 0.7 copy.122
  (19 shorter events, 3.0 us)
Async XLA Ops:
  7.2 32.8 %all-gather.5.cloned.1.call-start = ((), (), s32[]{:S(2)}) async-start(), calls=%async_computation.3 | async-start | bytes 1179648 | tf_op jit(solution)/shard_map/all_gather | solution.py:278
  7.9 66.3 %all-gather.3.cloned.1.call-start = ((), (), s32[]{:S(2)}) async-start(), calls=%async_computation.2 | async-start | bytes 4128768 | tf_op jit(solution)/shard_map/all_gather | solution.py:278
  10.8 187.3 %copy-start = (bf16[384,832]{1,0:T(8,128)(2,1)}, bf16[384,832]{1,0:T(8,128)(2,1)S(1)}, u32[]{:S(2)}) copy-start(bf16[384,832]{1,0:T(8,128)(2,1)S(1)} %copy.84.hid) | copy-start | bytes 1916932
  199.6 37.8 %all-to-all-start.1 = ((bf16[8,64,256]{2,1,0:T(8,128)(2,1)}), bf16[8,64,256]{2,1,0:T(8,128)(2,1)S(1)}, u32[]{:S(2)}, u32[]{:S(2)}) async-start(bf16[8,64,256]{2,1,0:T(8,128)(2,1)} %copy.91), calls=%async_computation.1 | async-start | bytes 524288 | tf_op jit(solution)/shard_map/all_to_all | solution.py:300
  237.4 124.3 %all-to-all-start = ((bf16[8,832,64]{1,2,0:T(8,128)(2,1)}), bf16[8,832,64]{1,2,0:T(8,128)(2,1)S(1)}, u32[]{:S(2)}, u32[]{:S(2)}) async-start(bf16[8,832,64]{1,2,0:T(8,128)(2,1)} %copy.88), calls=%async_computation | async-start | bytes 1835008 | tf_op jit(solution)/shard_map/all_to_all | solution.py:299
  358.5 4.7 %copy-start.1 = (bf16[384,256]{1,0:T(8,128)(2,1)S(1)}, bf16[384,256]{1,0:T(8,128)(2,1)}, u32[]{:S(2)}) copy-start(bf16[384,256]{1,0:T(8,128)(2,1)} %get-tuple-element.36) | copy-start | bytes 589828
Sparse Core Ops, SparseCore 0:
  9.9 30.1 all-gather.4
  41.8 32.3 all-gather.2

commit v2 on v1

v2 whole, which is shorter than its diff:
```python
import jax
import jax.numpy as jnp
from jax import lax
from jax.experimental import pallas as pl
from jax.experimental.pallas import tpu as pltpu
from jax.sharding import PartitionSpec as P

BLK = 128
MESH = pl.DeviceIdType.MESH
f32, bf16 = jnp.float32, jnp.bfloat16


def rem(a, n):
    return lax.rem(a, n)


def kernel(ids, lives, hid_t, w_hbm, a_ref, b_ref, grad, out, dh, dg, ug,
           hid, masked, Wp, Gg, Zs, Zr, Ys, Yr, Sown, acc, dacc,
           As, Ar, Bs, Br, Ts, Tr, Us, Ur, terms, uterms, part, part_r, fold, fold_r, act,
           lS, wS, wR, gS, gR, zS, zR, yS, yR, aS, aR, bS, bR, tS, tR, uS, uR, p1S, p1R, p2S, p2R, p3S, p3R):
    dp, mp = lax.axis_index("dp"), lax.axis_index("mp")
    x, c, y, z = dp // 2, rem(dp, 2), mp // 8, rem(mp, 8)

    def dev(dx=0, dc=0, dy=0, dz=0):
        return (rem(x + dx, 4) * 2 + rem(c + dc, 2), rem(y + dy, 4) * 8 + rem(z + dz, 8))

    XP, XM, SIB = dev(dx=1), dev(dx=3), dev(dc=1)
    YP, YM, Y2, ZP, ZM = dev(dy=1), dev(dy=3), dev(dy=2), dev(dz=1), dev(dz=7)

    bar = pltpu.get_barrier_semaphore()
    dps = [(rem(dp + k, 8), mp) for k in range(8)]
    ys = [dev(dy=k) for k in range(4)]
    zs = [dev(dz=k) for k in range(8)]
    peers = dps[1:] + ys[1:] + zs[1:]
    for p in peers:
        pl.semaphore_signal(bar, inc=1, device_id=p, device_id_type=MESH)

    wbase = x * 8 + c * 4
    loc = [pltpu.make_async_copy(w_hbm.at[:, pl.ds(256 * i, 256)], Wp.at[wbase + i], lS.at[i]) for i in range(4)]
    for cp in loc:
        cp.start()
    gslot = y * 8 + z
    gl = pltpu.make_async_copy(grad, Gg.at[gslot], lS.at[4])
    gl.start()

    def wanted(d):
        found, sel = jnp.int32(0), jnp.int32(0)
        for b in range(3):
            i = ids[3 * d + b]
            hit = (i // 4) == dp
            found = jnp.where(hit, 1, found)
            sel = jnp.where(hit, i % 4, sel)
        return found, sel

    own = [ids[3 * dp + b] // 4 for b in range(3)]

    def block_for(o):
        sel = jnp.int32(0)
        for b in range(1, 3):
            sel = jnp.where(own[b] == o, b, sel)
        return sel

    live = lives[dp]
    rows = lax.broadcasted_iota(jnp.int32, (384, 1), 0)
    for k in range(8):
        _, sel = wanted(dps[k][0])
        (Ar if k == 0 else As)[k] = a_ref[sel]
        (Br if k == 0 else Bs)[k] = b_ref[sel]
    hid[...] = hid_t[...].T
    masked[...] = jnp.where(rows < live, grad[...], jnp.zeros_like(grad))
    pl.semaphore_wait(bar, len(peers))

    sends = []

    def put(src, dst, ss, rs, to):
        cp = pltpu.make_async_remote_copy(src_ref=src, dst_ref=dst, send_sem=ss, recv_sem=rs, device_id=to, device_id_type=MESH)
        cp.start()
        sends.append(cp)

    def got(dst, ss, rs):
        pltpu.make_async_remote_copy(src_ref=dst, dst_ref=dst, send_sem=ss, recv_sem=rs, device_id=XP, device_id_type=MESH).wait_recv()

    def wsl(dx, i, n, dc=0):
        return Wp.at[pl.ds(rem(x + dx, 4) * 8 + rem(c + dc, 2) * 4 + i, n)]

    def wput(k, dx, i, n, to):
        put(wsl(dx, i, n), wsl(dx, i, n), wS.at[k], wR.at[k], to)

    def wgot(k, dx, i, n, dc=0):
        got(wsl(dx, i, n, dc), wS.at[k], wR.at[k])

    def gsl(dy, j, n):
        return Gg.at[pl.ds(rem(y + dy, 4) * 8 + j, n)]

    def gz(dz, lo=0, n=384):
        return Gg.at[y * 8 + rem(z + dz, 8), pl.ds(lo, n)]

    def gput(k, ref, to):
        put(ref, ref, gS.at[k], gR.at[k], to)

    for k in range(1, 8):
        put(Bs.at[k], Br.at[k], bS.at[k], bR.at[k], dps[k])
    for k in range(1, 8):
        put(As.at[k], Ar.at[k], aS.at[k], aR.at[k], dps[k])
    gl.wait()
    gput(0, gz(0), ZP)
    gput(1, gz(0), ZM)
    for cp in loc:
        cp.wait()
    wput(0, 0, 0, 2, XP)
    wput(2, 0, 2, 2, XM)
    wput(6, 0, 0, 4, SIB)
    wput(1, 0, 2, 2, XP)
    wput(3, 0, 0, 2, XM)

    def product(yt, zt):
        acc[...] = jnp.dot(hid[...], Wp[yt * 8 + zt], preferred_element_type=f32)

    def zcopy(r, slot, h, to):
        s = pltpu.make_async_remote_copy(
            src_ref=Zs.at[r, slot, h], dst_ref=Zr.at[r, slot, h], send_sem=zS.at[r, slot, h],
            recv_sem=zR.at[r, slot, h], device_id=to, device_id_type=MESH)
        return s

    def half(h):
        return acc[pl.ds(192 * h, 192)]

    def level0(r, yt):
        product(yt, rem(z + 4, 8))
        for h, to in ((0, ZM), (1, ZP)):
            Zs[r, 0, h] = half(h).astype(bf16)
            zcopy(r, 0, h, to).start()

    def level1(r, yt):
        for s, to in ((0, ZM), (1, ZP)):
            product(yt, rem(z + (5 if s == 0 else 3), 8))
            slot = 1 + s
            Zs[r, slot, 1 - s] = half(1 - s).astype(bf16)
            zcopy(r, slot, 1 - s, to).start()
            zcopy(r, 0, s, to).wait_recv()
            Zs[r, slot, s] = (half(s) + Zr[r, 0, s].astype(f32)).astype(bf16)
            zcopy(r, slot, s, to).start()

    def level23(r, yt, l):
        for s, to in ((0, ZM), (1, ZP)):
            product(yt, rem(z + (4 + l if s == 0 else 4 - l), 8))
            slot = 2 * l - 1 + s
            for h in (1 - s, s):
                zcopy(r, slot - 2, h, to).wait_recv()
                Zs[r, slot, h] = (half(h) + Zr[r, slot - 2, h].astype(f32)).astype(bf16)
                zcopy(r, slot, h, to).start()

    def ycopy(r, yt):
        j = rem(y - yt + 4, 4)
        return pltpu.make_async_remote_copy(
            src_ref=Ys.at[r], dst_ref=Yr.at[j - 1], send_sem=yS.at[r], recv_sem=yR.at[j - 1],
            device_id=(dp, yt * 8 + z), device_id_type=MESH)

    def level4(r, yt):
        product(yt, z)
        for h in (0, 1):
            for slot in (5, 6):
                zcopy(r, slot, h, ZP).wait_recv()
            acc[pl.ds(192 * h, 192)] = half(h) + (Zr[r, 5, h].astype(f32) + Zr[r, 6, h].astype(f32))

        @pl.when(y == yt)
        def _():
            Sown[...] = acc[...]

        @pl.when(y != yt)
        def _():
            Ys[r] = acc[...].astype(bf16)
            ycopy(r, yt).start()

    def back(m, n=2):
        g = jnp.concatenate([Gg[m + i] for i in range(n)], axis=1)
        w = jnp.concatenate([Wp[m + i] for i in range(n)], axis=1)
        dacc[...] += lax.dot_general(w, g, (((1,), (1,)), ((), ())), preferred_element_type=f32)

    def backs(yt):
        def b(i, _):
            back(yt * 8 + 2 * i)
            return 0
        lax.fori_loop(0, 4, b, 0)

    TB = (((1,), (1,)), ((), ()))
    TA = (((0,), (0,)), ((), ()))
    slot = [rem(dp - own[b] + 8, 8) for b in range(3)]

    def dslice(k, n=48):
        return pl.ds(pl.multiple_of(k * 48, 16), n)

    def rank_parts():
        for k in range(1, 8):
            got(Br.at[k], bS.at[k], bR.at[k])
        for k in range(1, 8):
            got(Ar.at[k], aS.at[k], aR.at[k])
        for b in range(3):
            r = pl.ds(128 * b, 128)
            dn = lax.dot_general(hid[r], Ar[slot[b]], TB, preferred_element_type=f32)
            up = lax.dot_general(masked[r], Br[slot[b]], TB, preferred_element_type=f32)
            part[r] = jnp.concatenate([dn, up], axis=1)
        for k in range(1, 8):
            put(part.at[dslice(rem(z + k, 8))], part_r.at[k], p1S.at[k], p1R.at[k], zs[k])

    def rank_fold_z():
        v = part[dslice(z)]
        for k in range(1, 8):
            got(part_r.at[k], p1S.at[k], p1R.at[k])
            v = v + part_r[k]
        fold[...] = v
        for k in range(1, 4):
            put(fold, fold_r.at[k], p2S.at[k], p2R.at[k], ys[k])

    def rank_fold_y():
        v = fold[...]
        for k in range(1, 4):
            got(fold_r.at[k], p2S.at[k], p2R.at[k])
            v = v + fold_r[k]
        act[dslice(z)] = v.astype(bf16)
        mine = act.at[dslice(z)]
        for k in range(1, 8):
            put(mine, mine, p3S.at[k], p3R.at[k], zs[k])

    def rank_terms():
        for k in range(1, 8):
            theirs = act.at[dslice(rem(z + 8 - k, 8))]
            got(theirs, p3S.at[k], p3R.at[k])
        for b in range(3):
            r = pl.ds(128 * b, 128)
            u = act[r]
            dn, up = u[:, :64], u[:, 64:]
            terms[b] = lax.dot_general(up, hid[r], TA, preferred_element_type=f32).astype(bf16)
            uterms[b] = lax.dot_general(dn, masked[r], TA, preferred_element_type=f32).astype(bf16)
        for k in range(8):
            sel = block_for(dps[k][0])
            (Tr if k == 0 else Ts)[k] = terms[sel]
            (Ur if k == 0 else Us)[k] = uterms[sel]
        for k in range(1, 8):
            put(Ts.at[k], Tr.at[k], tS.at[k], tR.at[k], dps[k])
            put(Us.at[k], Ur.at[k], uS.at[k], uR.at[k], dps[k])

    def rank_side():
        for b in range(3):
            up = act[pl.ds(128 * b, 128)][:, 64:]
            a_t = Ar[slot[b]].T
            dacc[:, pl.ds(128 * b, 128)] = lax.dot_general(a_t, up, TB, preferred_element_type=f32)

    def rank_out():
        for k in range(1, 8):
            got(Tr.at[k], tS.at[k], tR.at[k])
            got(Ur.at[k], uS.at[k], uR.at[k])
        picks = [wanted(rem(dp - k + 8, 8)) for k in range(8)]
        for a in range(4):
            w = [jnp.where((f == 1) & (s == a), 1.0, 0.0).astype(f32) for f, s in picks]
            v = w[0] * Tr[0].astype(f32)
            u = w[0] * Ur[0].astype(f32)
            for k in range(1, 8):
                v = v + w[k] * Tr[k].astype(f32)
                u = u + w[k] * Ur[k].astype(f32)
            dg[a] = v.astype(bf16)
            ug[a] = u.astype(bf16)

    y0, y1, y2, y3 = x, rem(x + 3, 4), rem(x + 1, 4), rem(x + 2, 4)

    wgot(6, 0, 0, 4, 1)
    level0(0, y0)
    got(gz(7), gS.at[0], gR.at[0]); gput(2, gz(7), ZP)
    got(gz(1), gS.at[1], gR.at[1]); gput(3, gz(1), ZM)
    level1(0, y0)
    rank_parts()
    got(gz(6), gS.at[2], gR.at[2]); gput(4, gz(6), ZP)
    got(gz(2), gS.at[3], gR.at[3]); gput(5, gz(2), ZM)
    level23(0, y0, 2)
    got(gz(5), gS.at[4], gR.at[4]); gput(6, gz(5, 0, 192), ZP)
    got(gz(3), gS.at[5], gR.at[5]); gput(7, gz(3, 192, 192), ZM)
    level23(0, y0, 3)
    got(gz(4, 0, 192), gS.at[6], gR.at[6])
    got(gz(4, 192, 192), gS.at[7], gR.at[7])
    gput(8, gsl(0, 0, 4), YP)
    gput(10, gsl(0, 4, 4), YM)
    gput(9, gsl(0, 4, 4), YP)
    gput(11, gsl(0, 0, 4), YM)
    level4(0, y0)
    rank_fold_z()

    wgot(0, 3, 0, 2); wput(4, 3, 0, 2, XP); wput(7, 3, 0, 2, SIB)
    wgot(2, 1, 2, 2); wput(5, 1, 2, 2, XM); wput(9, 1, 2, 2, SIB)
    wgot(1, 3, 2, 2); wput(8, 3, 2, 2, SIB)
    wgot(3, 1, 0, 2); wput(10, 1, 0, 2, SIB)
    wgot(7, 3, 0, 2, 1); wgot(8, 3, 2, 2, 1); wgot(9, 1, 2, 2, 1); wgot(10, 1, 0, 2, 1)

    rank_fold_y()

    def both(fn, *a):
        def b(i, _):
            fn(1 + i, rem(x + 3 - 2 * i, 4), *a)
            return 0
        lax.fori_loop(0, 2, b, 0)

    both(level0)
    both(level1)
    rank_terms()
    rank_side()
    both(level23, 2)
    got(gsl(3, 0, 4), gS.at[8], gR.at[8]); gput(12, gsl(3, 0, 4), YP)
    got(gsl(1, 4, 4), gS.at[10], gR.at[10]); gput(13, gsl(1, 4, 4), YM)
    both(level23, 3)
    both(level4)

    wgot(4, 2, 0, 2); wput(11, 2, 0, 2, SIB)
    wgot(5, 2, 2, 2); wput(12, 2, 2, 2, SIB)
    wgot(11, 2, 0, 2, 1); wgot(12, 2, 2, 2, 1)
    level0(3, y3)
    got(gsl(3, 4, 4), gS.at[9], gR.at[9])
    got(gsl(1, 0, 4), gS.at[11], gR.at[11])
    got(gsl(2, 0, 4), gS.at[12], gR.at[12])
    got(gsl(2, 4, 4), gS.at[13], gR.at[13])
    level1(3, y3)
    backs(y0)
    level23(3, y3, 2)
    backs(y1)
    level23(3, y3, 3)
    backs(y2)
    level4(3, y3)
    backs(y3)

    columns = lax.broadcasted_iota(jnp.int32, (1, 384), 1)
    dh[...] = jnp.where(columns < live, dacc[...], 0.0).astype(bf16)
    rank_out()
    for j in range(3):
        pltpu.make_async_remote_copy(src_ref=Yr.at[j], dst_ref=Yr.at[j], send_sem=yS.at[0], recv_sem=yR.at[j], device_id=XP, device_id_type=MESH).wait_recv()
    total = Sown[...] + (Yr[0].astype(f32) + Yr[1].astype(f32) + Yr[2].astype(f32))
    for b in range(3):
        r = pl.ds(128 * b, 128)
        branch = jnp.dot(act[r][:, :64], Br[slot[b]], preferred_element_type=f32)
        t = total[128 * b:128 * b + 128] + branch
        out[r] = jnp.where(rows[128 * b:128 * b + 128] < live, t, 0.0).astype(bf16)

    for cp in sends:
        cp.wait_send()

    def zw(i, _):
        r, slot = i // 7, rem(i, 7)
        for h in (0, 1):
            zcopy(r, slot, h, ZP).wait_send()
        return 0
    lax.fori_loop(0, 28, zw, 0)
    for r, yt in enumerate((y0, y1, y2, y3)):
        @pl.when(y != yt)
        def _():
            ycopy(r, yt).wait_send()


def shards(hidden, down_weight, adapter_down, adapter_up, output_grad, adapter_per_block, live_rows):
    V = pl.BlockSpec(memory_space=pltpu.VMEM)
    S = pl.BlockSpec(memory_space=pltpu.SMEM)
    D = pltpu.SemaphoreType.DMA
    M = pltpu.VMEM
    out, dh_t, dg_t, ug = pl.pallas_call(
        kernel,
        out_shape=(
            jax.ShapeDtypeStruct((384, 256), bf16), jax.ShapeDtypeStruct((832, 384), bf16),
            jax.ShapeDtypeStruct((4, 64, 832), bf16), jax.ShapeDtypeStruct((4, 64, 256), bf16)),
        in_specs=[S, S, V, pl.BlockSpec(memory_space=pl.ANY), V, V, V],
        out_specs=(V, V, V, V),
        scratch_shapes=[
            M((384, 832), bf16),
            M((384, 256), bf16),
            M((32, 832, 256), bf16),
            M((32, 384, 256), bf16),
            M((4, 7, 2, 192, 256), bf16),
            M((4, 7, 2, 192, 256), bf16),
            M((4, 384, 256), bf16),
            M((3, 384, 256), bf16),
            M((384, 256), f32),
            M((384, 256), f32),
            M((832, 384), f32),
            M((8, 64, 832), bf16), M((8, 64, 832), bf16), M((8, 64, 256), bf16), M((8, 64, 256), bf16),
            M((8, 64, 832), bf16), M((8, 64, 832), bf16), M((8, 64, 256), bf16), M((8, 64, 256), bf16),
            M((3, 64, 832), bf16), M((3, 64, 256), bf16),
            M((384, 128), f32), M((8, 48, 128), f32), M((48, 128), f32), M((4, 48, 128), f32), M((384, 128), bf16),
            D((5,)), D((13,)), D((13,)), D((14,)), D((14,)),
            D((4, 7, 2)), D((4, 7, 2)), D((4,)), D((3,)),
            D((8,)), D((8,)), D((8,)), D((8,)), D((8,)), D((8,)), D((8,)), D((8,)),
            D((8,)), D((8,)), D((4,)), D((4,)), D((8,)), D((8,)),
        ],
        name="layer",
        cost_estimate=pl.CostEstimate(flops=2 * 2 * 384 * 832 * 8192, bytes_accessed=6 * 2 ** 20, transcendentals=0),
        compiler_params=pltpu.CompilerParams(collective_id=0, has_side_effects=True, vmem_limit_bytes=58 * 2 ** 20),
    )(adapter_per_block, live_rows, hidden.T, down_weight, jnp.swapaxes(adapter_down, 1, 2), adapter_up, output_grad)
    return out, dh_t.T, jnp.swapaxes(dg_t, 1, 2), ug


def solution(mesh):
    return jax.shard_map(
        shards,
        mesh=mesh,
        in_specs=(P("dp", "mp"), P("mp", "dp"), P("dp", "mp", None), P("dp", None, "mp"), P("dp", "mp"), P(), P()),
        out_specs=(P("dp", "mp"), P("dp", "mp"), P("dp", "mp", None), P("dp", None, "mp")),
        check_vma=False,
    )
```

time: 374 us -> 163 us (0.44)
  blocking collectives: 117 us -> 0 us
  waiting for transfers between devices: 63.4 us -> 0 us
  Pallas kernels: 117 us -> 156 us
  starting transfers between devices: 35.8 us -> 0 us
  between operations: 14.1 us -> 0.66 us
  matrix products: 12.1 us -> 0 us
  local copies, waits for them, and re-layouts: 9.74 us -> 5.08 us
    psum x1 -> x0, blocking collectives: 117 us -> none  [shards(): down_sum, up_sum = lax.psum((down_part, up_part), 'mp')]
    all_gather x2 -> x0, waiting for transfers between devices: 58.1 us -> none  [the longest x1 32.1 us: shards(): lax.all_gather(adapter_down, 'dp', axis=0, tiled=True)]
    pallas_call x1, Pallas kernels: 117 us -> 156 us  [shards(): pl.pallas_call(kernel, out_shape=(jax.ShapeDtypeStruct((384, 256), bf16),...]
    all_to_all x2 -> x0, starting transfers between devices: 35.7 us -> none  [the longest x1 31.2 us: shards(): lax.all_to_all(back_up, 'dp', split_axis=0, concat_axis=0, tiled=True)]
    dot_general x12 -> x0, matrix products: 12.1 us -> none  [the longest x1 4.99 us: shards(): jnp.einsum('bk,kfr->bfr', select, every_down, preferred_element_type=jnp....]
    all_to_all x2 -> x0, waiting for transfers between devices: 3.89 us -> none  [the longest x1 3.88 us: shards(): lax.all_to_all(back_up, 'dp', split_axis=0, concat_axis=0, tiled=True)]
  transfers between devices with their start and end apart: 4 -> 0, of which waited for: 3 -> 0; matrix products, arithmetic and copies ran while one was open for 4% -> 0% of each run, Pallas kernels for 31% -> 0%
where the time goes in v2:
time: 163 us; the launch traced here: 162 us
  Pallas kernels  156 us (96%)
  local copies, waits for them, and re-layouts  5.08 us (3%)
    pallas_call x1, Pallas kernels, shards(): pl.pallas_call(kernel, out_shape=(jax.ShapeDtypeStruct((384, 256), bf16),...  156 us
    unnamed x8, local copies, waits for them, and re-layouts  5.08 us

profile of v2, /device:TPU:1, one launch (start us, length us, event | category | flops | bytes accessed | tf_op | source)
XLA Modules:
  0.0 162.1 jit_solution(1216747861705312812)
XLA Ops:
  0.6 156.4 %layer.1 = (bf16[384,256]{1,0:T(8,128)(2,1)}, bf16[832,384]{1,0:T(8,128)(2,1)}, bf16[4,64,832]{2,1,0:T(8,128)(2,1)}, bf16[4,64,256]{2,1,0:T(8,128)(2,1)}) custom-call(s32[24]{0:T(128)} %ids.1, s32[8]{0:T(128)} %lives.1, bf16[832,384]{1,0:T(8,128)(2,1)} %bitcast.6, bf16[832,1024]{1,0:T(8,128)(2,1)} %w_hbm.1, bf16[4,64,832]{2,1,0:T(8,128)(2,1)} %bitcast.7, ...), custom_call_target="tpu_custom_call" | custom-call | flops 10468982784 | bytes 6291456 | tf_op jit(solution)/shard_map/layer/pallas_call | solution.py:360
  157.0 0.0 copy-start
  157.0 0.0 copy-start.1
  157.0 1.7 %copy.15 = bf16[384,256]{1,0:T(8,128)(2,1)} copy(bf16[384,256]{1,0:T(8,128)(2,1)} %get-tuple-element.16) | data formatting | bytes 393216
  158.7 2.0 %copy.16 = bf16[384,832]{0,1:T(8,128)(2,1)} copy(bf16[384,832]{0,1:T(8,128)(2,1)} %bitcast.4) | data formatting | bytes 1277952
  160.7 0.0 copy-done
  160.7 0.8 copy.17
  161.5 0.0 copy-done.1
  161.5 0.7 copy.18
Async XLA Ops:
  157.0 3.7 %copy-start = (bf16[4,64,832]{2,1,0:T(8,128)(2,1)S(1)}, bf16[4,64,832]{2,1,0:T(8,128)(2,1)}, u32[]{:S(2)}) copy-start(bf16[4,64,832]{2,1,0:T(8,128)(2,1)} %get-tuple-element.10) | copy-start | bytes 1277956
  157.0 4.4 %copy-start.1 = (bf16[4,64,256]{2,1,0:T(8,128)(2,1)S(1)}, bf16[4,64,256]{2,1,0:T(8,128)(2,1)}, u32[]{:S(2)}) copy-start(bf16[4,64,256]{2,1,0:T(8,128)(2,1)} %get-tuple-element.19) | copy-start | bytes 393220

commit v3 on v0

v3 whole, which is shorter than its diff:
```python
import jax
import jax.numpy as jnp
from jax import lax
from jax.experimental import pallas as pl
from jax.experimental.pallas import tpu as pltpu
from jax.sharding import PartitionSpec as P

BLK = 128
MESH = pl.DeviceIdType.MESH
f32, bf16 = jnp.float32, jnp.bfloat16
TB = (((1,), (1,)), ((), ()))
TA = (((0,), (0,)), ((), ()))


def rem(a, n):
    return lax.rem(a, n)


def kernel(ids, lives, hid_h, w_hbm, a_h, b_h, grad_h, out, dh, dg, ug,
           hid_t, hid, grad, masked, a_ref, b_ref, Wp, Gg, Zs, Zr, Ys, Yr, Sown, acc, dacc,
           As, Ar, Bs, Br, Ts, Tr, Us, Ur, terms, uterms, part, part_r, fold, fold_r, act, down_act, up_act,
           lS, wS, wR, w1S, w1R, gS, gR, gyS, gyR, gfS, gfR, zS, zR, yS, yR,
           aS, aR, bS, bR, tS, tR, uS, uR, p1S, p1R, p2S, p2R, p3S, p3R):
    dp, mp = lax.axis_index("dp"), lax.axis_index("mp")
    x, c, y, z = dp // 2, rem(dp, 2), mp // 8, rem(mp, 8)

    def dev(dx=0, dc=0, dy=0, dz=0):
        return (rem(x + dx, 4) * 2 + rem(c + dc, 2), rem(y + dy, 4) * 8 + rem(z + dz, 8))

    XP, XM, SIB = dev(dx=1), dev(dx=3), dev(dc=1)
    dps = [(rem(dp + k, 8), mp) for k in range(8)]
    ys = [dev(dy=k) for k in range(4)]
    zs = [dev(dz=k) for k in range(8)]
    YP, YM, ZP, ZM = ys[1], ys[3], zs[1], zs[7]

    bar = pltpu.get_barrier_semaphore()
    peers = dps[1:] + ys[1:] + zs[1:]
    for p in peers:
        pl.semaphore_signal(bar, inc=1, device_id=p, device_id_type=MESH)

    wbase = x * 8 + c * 4
    loc = [pltpu.make_async_copy(s, d, lS.at[i]) for i, (s, d) in enumerate(
        [(b_h, b_ref), (grad_h, grad), (grad_h, Gg.at[y * 8 + z]), (a_h, a_ref), (hid_h, hid_t)]
        + [(w_hbm.at[:, pl.ds(256 * i, 256)], Wp.at[wbase + i]) for i in range(4)])]
    for cp in loc:
        cp.start()

    def wanted(d):
        found, sel = jnp.int32(0), jnp.int32(0)
        for b in range(3):
            i = ids[3 * d + b]
            hit = (i // 4) == dp
            found = jnp.where(hit, 1, found)
            sel = jnp.where(hit, i % 4, sel)
        return found, sel

    own = [ids[3 * dp + b] // 4 for b in range(3)]

    def block_for(o):
        sel = jnp.int32(0)
        for b in range(1, 3):
            sel = jnp.where(own[b] == o, b, sel)
        return sel

    live = lives[dp]
    rows = lax.broadcasted_iota(jnp.int32, (384, 1), 0)
    slot = [rem(dp - own[b] + 8, 8) for b in range(3)]
    sels = [wanted(dps[k][0])[1] for k in range(8)]

    sends = []

    def put(src, dst, ss, rs, to):
        cp = pltpu.make_async_remote_copy(src_ref=src, dst_ref=dst, send_sem=ss, recv_sem=rs, device_id=to, device_id_type=MESH)
        cp.start()
        sends.append(cp)

    def got(dst, ss, rs):
        pltpu.make_async_remote_copy(src_ref=dst, dst_ref=dst, send_sem=ss, recv_sem=rs, device_id=XP, device_id_type=MESH).wait_recv()

    def wsl(dx, i, n, dc=0):
        return Wp.at[pl.ds(rem(x + dx, 4) * 8 + rem(c + dc, 2) * 4 + i, n)]

    def wput(k, dx, i, n, to):
        put(wsl(dx, i, n), wsl(dx, i, n), wS.at[k], wR.at[k], to)

    def wgot(k, dx, i, n, dc=0):
        got(wsl(dx, i, n, dc), wS.at[k], wR.at[k])

    ORDER = (0, 7, 1, 6, 2, 5, 3, 4)

    def gsl(dy, dz, lo=0, n=384):
        return Gg.at[rem(y + dy, 4) * 8 + rem(z + dz, 8), pl.ds(lo, n)]

    def gput(k, ref, to):
        put(ref, ref, gS.at[k], gR.at[k], to)

    def gz(k):
        if k < 4:
            lo, hi = gsl(0, 8 - k), gsl(0, k)
            got(lo, gS.at[2 * k - 2], gR.at[2 * k - 2])
            got(hi, gS.at[2 * k - 1], gR.at[2 * k - 1])
            if k == 3:
                lo, hi = gsl(0, 5, 0, 192), gsl(0, 3, 192, 192)
            gput(2 * k, lo, ZP)
            gput(2 * k + 1, hi, ZM)
        else:
            got(gsl(0, 4, 0, 192), gS.at[6], gR.at[6])
            got(gsl(0, 4, 192, 192), gS.at[7], gR.at[7])

    def gy(j):
        ref = gsl(0, ORDER[j])
        put(ref, ref, gyS.at[j, 0], gyR.at[j, 0], YP)
        put(ref, ref, gyS.at[j, 1], gyR.at[j, 1], YM)

    def gf(j):
        got(gsl(3, ORDER[j]), gyS.at[j, 0], gyR.at[j, 0])
        ref = gsl(3, ORDER[j], 0, 192)
        put(ref, ref, gfS.at[j, 0], gfR.at[j, 0], YP)
        got(gsl(1, ORDER[j]), gyS.at[j, 1], gyR.at[j, 1])
        ref = gsl(1, ORDER[j], 192, 192)
        put(ref, ref, gfS.at[j, 1], gfR.at[j, 1], YM)

    def gl(j):
        got(gsl(2, ORDER[j], 0, 192), gfS.at[j, 0], gfR.at[j, 0])
        got(gsl(2, ORDER[j], 192, 192), gfS.at[j, 1], gfR.at[j, 1])

    def row(r, zt):
        if r in (0, 3):
            return rem(x + (0 if r == 0 else 2), 4)
        left = rem(zt, 4) < 2
        return rem(x + jnp.where(left, 3, 1) if r == 1 else x + jnp.where(left, 1, 3), 4)

    def pre(r, level):
        b = r // 3
        if level in (0, 4):
            zt = rem(z + 4, 8) if level == 0 else z
            acc[b, 0] = jnp.dot(hid[...], Wp[row(r, zt) * 8 + zt], preferred_element_type=f32)
            return
        for s in (0, 1):
            zt = rem(z + (4 + level if s == 0 else 4 - level), 8)
            acc[b, s] = jnp.dot(hid[...], Wp[row(r, zt) * 8 + zt], preferred_element_type=f32)

    def zcopy(r, k, h, to):
        return pltpu.make_async_remote_copy(
            src_ref=Zs.at[r, k, h], dst_ref=Zr.at[r, k, h], send_sem=zS.at[r, k, h],
            recv_sem=zR.at[r, k, h], device_id=to, device_id_type=MESH)

    def half(r, s, h):
        return acc[r // 3, s, pl.ds(192 * h, 192)]

    def send(r, k, h, to, v):
        Zs[r, k, h] = v.astype(bf16)
        zcopy(r, k, h, to).start()

    def level0(r):
        for h, to in ((0, ZM), (1, ZP)):
            send(r, 0, h, to, half(r, 0, h))

    def level1(r):
        for s, to in ((0, ZM), (1, ZP)):
            send(r, 1 + s, 1 - s, to, half(r, s, 1 - s))
        for s, to in ((0, ZM), (1, ZP)):
            zcopy(r, 0, s, to).wait_recv()
            send(r, 1 + s, s, to, half(r, s, s) + Zr[r, 0, s].astype(f32))

    def level23(r, l):
        for i in (0, 1):
            for s, to in ((0, ZM), (1, ZP)):
                k, h = 2 * l - 1 + s, (1 - s if i == 0 else s)
                zcopy(r, k - 2, h, to).wait_recv()
                send(r, k, h, to, half(r, s, h) + Zr[r, k - 2, h].astype(f32))

    def level(r, l):
        if l == 0:
            level0(r)
        elif l == 1:
            level1(r)
        elif l < 4:
            level23(r, l)
        else:
            level4(r)

    def both(r, l):
        pre(r, l)
        level(r, l)

    def ycopy(r, h):
        yt = row(r, z)
        j = rem(y - yt + 4, 4)
        return pltpu.make_async_remote_copy(
            src_ref=Ys.at[r, h], dst_ref=Yr.at[j - 1, h], send_sem=yS.at[r, h], recv_sem=yR.at[j - 1, h],
            device_id=(dp, yt * 8 + z), device_id_type=MESH)

    def level4(r):
        for h in (0, 1):
            for k in (5, 6):
                zcopy(r, k, h, ZP).wait_recv()
            v = half(r, 0, h) + (Zr[r, 5, h].astype(f32) + Zr[r, 6, h].astype(f32))
            Ys[r, h] = v.astype(bf16)

            @pl.when(y == row(r, z))
            def _():
                Sown[pl.ds(192 * h, 192)] = v

            @pl.when(y != row(r, z))
            def _():
                ycopy(r, h).start()

    def backs(yt, lo=0, n=4):
        def b(i, _):
            m = yt * 8 + 2 * (i + lo)
            g = jnp.concatenate([Gg[m], Gg[m + 1]], axis=1)
            w = jnp.concatenate([Wp[m], Wp[m + 1]], axis=1)
            dacc[...] += lax.dot_general(w, g, TB, preferred_element_type=f32)
            return 0
        lax.fori_loop(0, n, b, 0)

    def piece(k):
        return pl.ds(pl.multiple_of(rem(z + k, 8) * 24, 8), 24)

    def scatter(i, blocks):
        v = jnp.concatenate(blocks, axis=0)
        part[i] = jnp.concatenate([v[:192], v[192:]], axis=1)
        for k in range(1, 8):
            put(part.at[i, piece(k)], part_r.at[i, k], p1S.at[i, k], p1R.at[i, k], zs[k])

    def fold_z(i):
        v = part[i, piece(0)]
        for k in range(1, 8):
            got(part_r.at[i, k], p1S.at[i, k], p1R.at[i, k])
            v = v + part_r[i, k]
        fold[i] = v
        for k in range(1, 4):
            put(fold.at[i], fold_r.at[i, k], p2S.at[i, k], p2R.at[i, k], ys[k])

    def fold_y(i):
        v = fold[i]
        for k in range(1, 4):
            got(fold_r.at[i, k], p2S.at[i, k], p2R.at[i, k])
            v = v + fold_r[i, k]
        act[i, piece(0)] = v
        mine = act.at[i, piece(0)]
        for k in range(1, 8):
            put(mine, mine, p3S.at[i, k], p3R.at[i, k], zs[k])

    def gather(i, to):
        for k in range(1, 8):
            got(act.at[i, piece(8 - k)], p3S.at[i, k], p3R.at[i, k])
        v = act[i].astype(bf16)
        to[...] = jnp.concatenate([v[:, :64], v[:, 64:]], axis=0)

    def blk(b):
        return pl.ds(128 * b, 128)

    def up_scatter():
        for k in range(1, 8):
            got(Br.at[k], bS.at[k], bR.at[k])
        scatter(1, [lax.dot_general(masked[blk(b)], Br[slot[b]], TB, preferred_element_type=f32) for b in range(3)])

    def down_scatter():
        for k in range(1, 8):
            got(Ar.at[k], aS.at[k], aR.at[k])
        scatter(0, [lax.dot_general(hid[blk(b)], Ar[slot[b]], TB, preferred_element_type=f32) for b in range(3)])

    def up_terms():
        gather(1, up_act)
        for b in range(3):
            terms[b] = lax.dot_general(up_act[blk(b)], hid[blk(b)], TA, preferred_element_type=f32).astype(bf16)
        for k in range(8):
            (Tr if k == 0 else Ts)[k] = terms[block_for(dps[k][0])]
        for k in range(1, 8):
            put(Ts.at[k], Tr.at[k], tS.at[k], tR.at[k], dps[k])

    def down_terms():
        gather(0, down_act)
        for b in range(3):
            uterms[b] = lax.dot_general(down_act[blk(b)], masked[blk(b)], TA, preferred_element_type=f32).astype(bf16)
        for k in range(8):
            (Ur if k == 0 else Us)[k] = uterms[block_for(dps[k][0])]
        for k in range(1, 8):
            put(Us.at[k], Ur.at[k], uS.at[k], uR.at[k], dps[k])

    def side():
        for b in range(3):
            dacc[:, blk(b)] += lax.dot_general(Ar[slot[b]].T, up_act[blk(b)], TB, preferred_element_type=f32)

    def owned(recv, ss, rs, to):
        for k in range(1, 8):
            got(recv.at[k], ss.at[k], rs.at[k])
        picks = [wanted(rem(dp - k + 8, 8)) for k in range(8)]
        for a in range(4):
            v = None
            for k, (found, sel) in enumerate(picks):
                w = jnp.where((found == 1) & (sel == a), 1.0, 0.0).astype(f32)
                t = w * recv[k].astype(f32)
                v = t if v is None else v + t
            to[a] = v.astype(bf16)

    loc[0].wait()
    for k in range(8):
        (Br if k == 0 else Bs)[k] = b_ref[sels[k]]
    pl.semaphore_wait(bar, len(peers))
    def first(d, i):
        put(w_hbm.at[:, pl.ds(256 * i, 256)], Wp.at[wbase + i], w1S.at[d, i], w1R.at[d, i], (XP, XM)[d])

    def came(d, i):
        got(wsl(3 if d == 0 else 1, i, 1), w1S.at[d, i], w1R.at[d, i])

    first(0, 0); first(1, 2); first(0, 1); first(1, 3)
    loc[2].wait()
    gput(0, gsl(0, 0), ZP)
    gput(1, gsl(0, 0), ZM)
    gy(0)
    for k in range(1, 8):
        put(Bs.at[k], Br.at[k], bS.at[k], bR.at[k], dps[k])
    for cp in loc[5:]:
        cp.wait()
    wput(6, 0, 0, 4, SIB)
    first(0, 2); first(1, 0); first(0, 3); first(1, 1)
    loc[1].wait()
    masked[...] = jnp.where(rows < live, grad[...], jnp.zeros_like(grad))
    loc[3].wait()
    for k in range(8):
        (Ar if k == 0 else As)[k] = a_ref[sels[k]]
    dacc[...] = jnp.zeros_like(dacc)
    loc[4].wait()
    hid[...] = hid_t[...].T

    far = rem(y - x + 4, 4)
    r1 = rem(x + jnp.where(far == 2, 1, 0), 4)
    r2 = rem(x + jnp.where(far < 2, 1, 3), 4)
    r3 = rem(x + jnp.where(far < 2, 3, far - 2), 4)
    r4 = rem(x + 2, 4)

    wgot(6, 0, 0, 4, 1)
    both(0, 0)
    gz(1); gy(1); gy(2)
    both(0, 1)
    gz(2); gy(3); gy(4)
    both(0, 2)
    gz(3); gy(5); gy(6)
    came(0, 0); wput(4, 3, 0, 1, XP); came(0, 1); wput(5, 3, 1, 1, XP); wput(7, 3, 0, 2, SIB)
    came(1, 2); wput(13, 1, 2, 1, XM); came(1, 3); wput(14, 1, 3, 1, XM); wput(9, 1, 2, 2, SIB)
    for k in range(1, 8):
        put(As.at[k], Ar.at[k], aS.at[k], aR.at[k], dps[k])
    both(0, 3)
    up_scatter()
    wgot(7, 3, 0, 2, 1); wgot(9, 1, 2, 2, 1)
    both(1, 0)
    gz(4); gy(7)
    both(0, 4)
    fold_z(1)
    both(1, 1)
    gf(0); gf(1); gf(2)
    both(1, 2)
    fold_y(1)
    gf(3); gf(4)
    both(1, 3)
    gf(5); gf(6)
    came(0, 2); came(0, 3); wput(8, 3, 2, 2, SIB)
    came(1, 0); came(1, 1); wput(10, 1, 0, 2, SIB)
    up_terms()
    wgot(8, 3, 2, 2, 1); wgot(10, 1, 0, 2, 1)
    both(2, 0)
    gf(7)
    both(1, 4)
    backs(r1)
    both(2, 1)
    backs(r2)
    both(2, 2)
    wgot(4, 2, 0, 1); wput(11, 2, 0, 1, SIB)
    wgot(13, 2, 2, 1); wput(12, 2, 2, 1, SIB)
    both(2, 3)
    wgot(5, 2, 1, 1); wput(15, 2, 1, 1, SIB)
    wgot(14, 2, 3, 1); wput(16, 2, 3, 1, SIB)
    both(2, 4)
    wgot(11, 2, 0, 1, 1); wgot(12, 2, 2, 1, 1); wgot(15, 2, 1, 1, 1); wgot(16, 2, 3, 1, 1)
    both(3, 0)
    pre(3, 1)
    for j in range(8):
        gl(j)
    backs(r3)
    level(3, 1)
    pre(3, 2)
    down_scatter()
    level(3, 2)
    fold_z(0)
    pre(3, 3)
    backs(r4, 0, 2)
    level(3, 3)
    fold_y(0)
    pre(3, 4)
    backs(r4, 2, 2)
    level(3, 4)
    down_terms()
    side()
    columns = lax.broadcasted_iota(jnp.int32, (1, 384), 1)
    dh[...] = jnp.where(columns < live, dacc[...], 0.0).astype(bf16)
    owned(Tr, tS, tR, dg)
    for b in range(3):
        acc[0, 0, blk(b)] = jnp.dot(down_act[blk(b)], Br[slot[b]], preferred_element_type=f32)
    for h in (0, 1):
        r = pl.ds(192 * h, 192)
        for j in range(3):
            got(Yr.at[j, h], yS.at[0, h], yR.at[j, h])
        t = acc[0, 0, r] + Sown[r]
        for j in range(3):
            t = t + Yr[j, h].astype(f32)
        out[r] = jnp.where(rows[192 * h:192 * h + 192] < live, t, 0.0).astype(bf16)

    owned(Ur, uS, uR, ug)
    for cp in sends:
        cp.wait_send()

    def zw(i, _):
        for h in (0, 1):
            zcopy(i // 7, rem(i, 7), h, ZP).wait_send()
        return 0
    lax.fori_loop(0, 28, zw, 0)
    for r in range(4):
        @pl.when(y != row(r, z))
        def _():
            for h in (0, 1):
                ycopy(r, h).wait_send()


def finish(a, b, c, d, oa, ob, oc, od, sems):
    cps = [pltpu.make_async_copy(i, o, sems.at[k]) for k, (i, o) in enumerate(((a, oa), (b, ob), (c, oc), (d, od)))]
    for cp in cps:
        cp.start()
    for cp in cps:
        cp.wait()


def shards(hidden, down_weight, adapter_down, adapter_up, output_grad, adapter_per_block, live_rows):
    V = pl.BlockSpec(memory_space=pltpu.VMEM)
    S = pl.BlockSpec(memory_space=pltpu.SMEM)
    A = pl.BlockSpec(memory_space=pl.ANY)
    D = pltpu.SemaphoreType.DMA
    M = pltpu.VMEM
    out, dh_t, dg_t, ug = pl.pallas_call(
        kernel,
        out_shape=(
            jax.ShapeDtypeStruct((384, 256), bf16), jax.ShapeDtypeStruct((832, 384), bf16),
            jax.ShapeDtypeStruct((4, 64, 832), bf16), jax.ShapeDtypeStruct((4, 64, 256), bf16)),
        in_specs=[S, S, A, A, A, A, A],
        out_specs=(V, V, V, V),
        scratch_shapes=[
            M((832, 384), bf16), M((384, 832), bf16), M((384, 256), bf16), M((384, 256), bf16),
            M((4, 64, 832), bf16), M((4, 64, 256), bf16),
            M((32, 832, 256), bf16),
            M((32, 384, 256), bf16),
            M((4, 7, 2, 192, 256), bf16),
            M((4, 7, 2, 192, 256), bf16),
            M((4, 2, 192, 256), bf16),
            M((3, 2, 192, 256), bf16),
            M((384, 256), f32),
            M((2, 2, 384, 256), f32),
            M((832, 384), f32),
            M((8, 64, 832), bf16), M((8, 64, 832), bf16), M((8, 64, 256), bf16), M((8, 64, 256), bf16),
            M((8, 64, 832), bf16), M((8, 64, 832), bf16), M((8, 64, 256), bf16), M((8, 64, 256), bf16),
            M((3, 64, 832), bf16), M((3, 64, 256), bf16),
            M((2, 192, 128), f32), M((2, 8, 24, 128), f32), M((2, 24, 128), f32), M((2, 4, 24, 128), f32), M((2, 192, 128), f32),
            M((384, 64), bf16), M((384, 64), bf16),
            D((9,)), D((17,)), D((17,)), D((2, 4)), D((2, 4)), D((8,)), D((8,)), D((8, 2)), D((8, 2)), D((8, 2)), D((8, 2)),
            D((4, 7, 2)), D((4, 7, 2)), D((4, 2)), D((3, 2)),
            D((8,)), D((8,)), D((8,)), D((8,)), D((8,)), D((8,)), D((8,)), D((8,)),
            D((2, 8)), D((2, 8)), D((2, 4)), D((2, 4)), D((2, 8)), D((2, 8)),
        ],
        name="layer",
        cost_estimate=pl.CostEstimate(flops=2 * 2 * 384 * 832 * 8192, bytes_accessed=6 * 2 ** 20, transcendentals=0),
        compiler_params=pltpu.CompilerParams(collective_id=0, has_side_effects=True, vmem_limit_bytes=58 * 2 ** 20),
    )(adapter_per_block, live_rows, hidden.T, down_weight, jnp.swapaxes(adapter_down, 1, 2), adapter_up, output_grad)
    parts = (out, dh_t, dg_t, ug)
    out, dh_t, dg_t, ug = pl.pallas_call(
        finish,
        out_shape=tuple(jax.ShapeDtypeStruct(v.shape, v.dtype) for v in parts),
        in_specs=[A] * 4, out_specs=(A,) * 4, scratch_shapes=[D((4,))], name="finish",
        cost_estimate=pl.CostEstimate(flops=0, bytes_accessed=4 * 2 ** 20, transcendentals=0),
    )(*parts)
    return out, dh_t.T, jnp.swapaxes(dg_t, 1, 2), ug


def solution(mesh):
    return jax.shard_map(
        shards,
        mesh=mesh,
        in_specs=(P("dp", "mp"), P("mp", "dp"), P("dp", "mp", None), P("dp", None, "mp"), P("dp", "mp"), P(), P()),
        out_specs=(P("dp", "mp"), P("dp", "mp"), P("dp", "mp", None), P("dp", None, "mp")),
        check_vma=False,
    )
```

time: 497 us -> 163 us (0.33)
  waiting for transfers between devices: 277 us -> 0 us
  Pallas kernels: 0 us -> 163 us
  blocking collectives: 118 us -> 0 us
  matrix products: 36.4 us -> 0 us
  starting transfers between devices: 35.8 us -> 0 us
  between operations: 13.9 us -> 0.8 us
  local copies, waits for them, and re-layouts: 7.66 us -> 0 us
    pallas_call x0 -> x2, Pallas kernels: none -> 163 us  [the longest x1 118 us: shards(): pl.pallas_call(kernel, out_shape=(jax.ShapeDtypeStruct((384, 256), bf16),...]
    reduce_scatter x1 -> x0, waiting for transfers between devices: 138 us -> none  [shards(): lax.psum_scatter(partial_value, 'mp', scatter_dimension=1, tiled=True)]
    all_gather x4 -> x0, waiting for transfers between devices: 121 us -> none  [the longest x1 75.2 us: shards(): panel = lax.all_gather(down_weight, 'dp', axis=1, tiled=True)]
    psum x1 -> x0, blocking collectives: 118 us -> none  [shards(): down_sum, up_sum = lax.psum((down_part, up_part), 'mp')]
    dot_general x14 -> x0, matrix products: 36.4 us -> none  [the longest x1 13.5 us: shards(): lax.dot_general(grad_full, panel, (((1,), (1,)), ((), ())), preferred_ele...]
    all_to_all x2 -> x0, starting transfers between devices: 35.6 us -> none  [the longest x1 31.1 us: shards(): lax.all_to_all(back_up, 'dp', split_axis=0, concat_axis=0, tiled=True)]
    all_to_all x2 -> x0, waiting for transfers between devices: 15.2 us -> none  [the longest x1 10.6 us: shards(): lax.all_to_all(back_down, 'dp', split_axis=0, concat_axis=0, tiled=True)]
  transfers between devices with their start and end apart: 7 -> 0, of which waited for: 6 -> 0; matrix products, arithmetic and copies ran while one was open for 9% -> 0% of each run, Pallas kernels for 0% -> 0%
where the time goes in v3:
time: 163 us
  Pallas kernels  163 us (100%)
    pallas_call x1, Pallas kernels, shards(): pl.pallas_call(kernel, out_shape=(jax.ShapeDtypeStruct((384, 256), bf16),...  118 us
    pallas_call x1, Pallas kernels, shards(): pl.pallas_call(finish, out_shape=tuple((jax.ShapeDtypeStruct(v.shape, v.d...  44.3 us

profile of v3, /device:TPU:1, one launch (start us, length us, event | category | flops | bytes accessed | tf_op | source)
XLA Modules:
  0.0 163.3 jit_solution(13444964371053815323)
XLA Ops:
  0.6 118.2 %layer.1 = (bf16[384,256]{1,0:T(8,128)(2,1)}, bf16[832,384]{1,0:T(8,128)(2,1)}, bf16[4,64,832]{2,1,0:T(8,128)(2,1)}, bf16[4,64,256]{2,1,0:T(8,128)(2,1)}) custom-call(s32[24]{0:T(128)} %ids.1, s32[8]{0:T(128)} %lives.1, bf16[832,384]{1,0:T(8,128)(2,1)} %bitcast.4, bf16[832,1024]{1,0:T(8,128)(2,1)} %w_hbm.1, bf16[4,64,832]{2,1,0:T(8,128)(2,1)} %bitcast.6, ...), custom_call_target="tpu_custom_call" | custom-call | flops 10468982784 | bytes 6291456 | tf_op jit(solution)/shard_map/layer/pallas_call | solution.py:441
  118.8 44.3 %finish.1 = (bf16[384,256]{1,0:T(8,128)(2,1)}, bf16[832,384]{1,0:T(8,128)(2,1)}, bf16[4,64,832]{2,1,0:T(8,128)(2,1)}, bf16[4,64,256]{2,1,0:T(8,128)(2,1)}) custom-call(bf16[384,256]{1,0:T(8,128)(2,1)} %get-tuple-element.12.a, bf16[832,384]{1,0:T(8,128)(2,1)} %get-tuple-element.13.b, bf16[4,64,832]{2,1,0:T(8,128)(2,1)} %get-tuple-element.14.c, ...), custom_call_target="tpu_custom_call" | custom-call | bytes 4194304 | tf_op jit(solution)/shard_map/finish/pallas_call | solution.py:475

commit v4 on v3

--- a/solution.py
+++ b/solution.py
@@ -16,7 +16,7 @@
     return lax.rem(a, n)
 
 
-def kernel(ids, lives, hid_h, w_hbm, a_h, b_h, grad_h, out, dh, dg, ug,
+def kernel(ids, lives, hid_h, w_hbm, a_h, b_h, grad_h, out_h, dh_h, dg_h, ug_h, out, dh, dg, ug, oS,
            hid_t, hid, grad, masked, a_ref, b_ref, Wp, Gg, Zs, Zr, Ys, Yr, Sown, acc, dacc,
            As, Ar, Bs, Br, Ts, Tr, Us, Ur, terms, uterms, part, part_r, fold, fold_r, act, down_act, up_act,
            lS, wS, wR, w1S, w1R, gS, gR, gyS, gyR, gfS, gfR, zS, zR, yS, yR,
@@ -54,25 +54,23 @@
             sel = jnp.where(hit, i % 4, sel)
         return found, sel
 
-    own = [ids[3 * dp + b] // 4 for b in range(3)]
-
     def block_for(o):
         sel = jnp.int32(0)
         for b in range(1, 3):
             sel = jnp.where(own[b] == o, b, sel)
         return sel
 
-    live = lives[dp]
-    rows = lax.broadcasted_iota(jnp.int32, (384, 1), 0)
-    slot = [rem(dp - own[b] + 8, 8) for b in range(3)]
-    sels = [wanted(dps[k][0])[1] for k in range(8)]
 
     sends = []
 
-    def put(src, dst, ss, rs, to):
+    def put(src, dst, ss, rs, to, record=True):
         cp = pltpu.make_async_remote_copy(src_ref=src, dst_ref=dst, send_sem=ss, recv_sem=rs, device_id=to, device_id_type=MESH)
         cp.start()
-        sends.append(cp)
+        if record:
+            sends.append(cp)
+
+    def left(ref, ss):
+        pltpu.make_async_remote_copy(src_ref=ref, dst_ref=ref, send_sem=ss, recv_sem=ss, device_id=XP, device_id_type=MESH).wait_send()
 
     def got(dst, ss, rs):
         pltpu.make_async_remote_copy(src_ref=dst, dst_ref=dst, send_sem=ss, recv_sem=rs, device_id=XP, device_id_type=MESH).wait_recv()
@@ -109,20 +107,19 @@
 
     def gy(j):
         ref = gsl(0, ORDER[j])
-        put(ref, ref, gyS.at[j, 0], gyR.at[j, 0], YP)
-        put(ref, ref, gyS.at[j, 1], gyR.at[j, 1], YM)
+        put(ref, ref, gyS.at[0], gyR.at[j, 0], YP, False)
+        put(ref, ref, gyS.at[0], gyR.at[j, 1], YM, False)
 
     def gf(j):
-        got(gsl(3, ORDER[j]), gyS.at[j, 0], gyR.at[j, 0])
+        got(gsl(3, ORDER[j]), gyS.at[0], gyR.at[j, 0])
         ref = gsl(3, ORDER[j], 0, 192)
-        put(ref, ref, gfS.at[j, 0], gfR.at[j, 0], YP)
-        got(gsl(1, ORDER[j]), gyS.at[j, 1], gyR.at[j, 1])
+        put(ref, ref, gfS.at[0], gfR.at[0], YP, False)
+        got(gsl(1, ORDER[j]), gyS.at[0], gyR.at[j, 1])
         ref = gsl(1, ORDER[j], 192, 192)
-        put(ref, ref, gfS.at[j, 1], gfR.at[j, 1], YM)
-
-    def gl(j):
-        got(gsl(2, ORDER[j], 0, 192), gfS.at[j, 0], gfR.at[j, 0])
-        got(gsl(2, ORDER[j], 192, 192), gfS.at[j, 1], gfR.at[j, 1])
+        put(ref, ref, gfS.at[0], gfR.at[0], YM, False)
+
+    def gl():
+        got(Gg.at[pl.ds(rem(y + 2, 4) * 8, 8)], gfS.at[0], gfR.at[0])
 
     def row(r, zt):
         if r in (0, 3):
@@ -142,7 +139,7 @@
 
     def zcopy(r, k, h, to):
         return pltpu.make_async_remote_copy(
-            src_ref=Zs.at[r, k, h], dst_ref=Zr.at[r, k, h], send_sem=zS.at[r, k, h],
+            src_ref=Zs.at[r, k, h], dst_ref=Zr.at[r, k, h], send_sem=zS.at[r],
             recv_sem=zR.at[r, k, h], device_id=to, device_id_type=MESH)
 
     def half(r, s, h):
@@ -222,30 +219,29 @@
         v = jnp.concatenate(blocks, axis=0)
         part[i] = jnp.concatenate([v[:192], v[192:]], axis=1)
         for k in range(1, 8):
-            put(part.at[i, piece(k)], part_r.at[i, k], p1S.at[i, k], p1R.at[i, k], zs[k])
+            put(part.at[i, piece(k)], part_r.at[i, k], p1S.at[i], p1R.at[i], zs[k], False)
 
     def fold_z(i):
         v = part[i, piece(0)]
+        got(part_r.at[i, pl.ds(1, 7)], p1S.at[i], p1R.at[i])
         for k in range(1, 8):
-            got(part_r.at[i, k], p1S.at[i, k], p1R.at[i, k])
             v = v + part_r[i, k]
         fold[i] = v
         for k in range(1, 4):
-            put(fold.at[i], fold_r.at[i, k], p2S.at[i, k], p2R.at[i, k], ys[k])
+            put(fold.at[i], fold_r.at[i, k], p2S.at[i], p2R.at[i], ys[k], False)
 
     def fold_y(i):
         v = fold[i]
+        got(fold_r.at[i, pl.ds(1, 3)], p2S.at[i], p2R.at[i])
         for k in range(1, 4):
-            got(fold_r.at[i, k], p2S.at[i, k], p2R.at[i, k])
             v = v + fold_r[i, k]
         act[i, piece(0)] = v
         mine = act.at[i, piece(0)]
         for k in range(1, 8):
-            put(mine, mine, p3S.at[i, k], p3R.at[i, k], zs[k])
+            put(mine, mine, p3S.at[i], p3R.at[i], zs[k], False)
 
     def gather(i, to):
-        for k in range(1, 8):
-            got(act.at[i, piece(8 - k)], p3S.at[i, k], p3R.at[i, k])
+        got(act.at[i, pl.ds(0, 168)], p3S.at[i], p3R.at[i])
         v = act[i].astype(bf16)
         to[...] = jnp.concatenate([v[:, :64], v[:, 64:]], axis=0)
 
@@ -253,13 +249,11 @@
         return pl.ds(128 * b, 128)
 
     def up_scatter():
-        for k in range(1, 8):
-            got(Br.at[k], bS.at[k], bR.at[k])
+        got(Br.at[pl.ds(1, 7)], bS.at[0], bR.at[0])
         scatter(1, [lax.dot_general(masked[blk(b)], Br[slot[b]], TB, preferred_element_type=f32) for b in range(3)])
 
     def down_scatter():
-        for k in range(1, 8):
-            got(Ar.at[k], aS.at[k], aR.at[k])
+        got(Ar.at[pl.ds(1, 7)], aS.at[0], aR.at[0])
         scatter(0, [lax.dot_general(hid[blk(b)], Ar[slot[b]], TB, preferred_element_type=f32) for b in range(3)])
 
     def up_terms():
@@ -269,7 +263,7 @@
         for k in range(8):
             (Tr if k == 0 else Ts)[k] = terms[block_for(dps[k][0])]
         for k in range(1, 8):
-            put(Ts.at[k], Tr.at[k], tS.at[k], tR.at[k], dps[k])
+            put(Ts.at[k], Tr.at[k], tS.at[0], tR.at[0], dps[k], False)
 
     def down_terms():
         gather(0, down_act)
@@ -278,15 +272,14 @@
         for k in range(8):
             (Ur if k == 0 else Us)[k] = uterms[block_for(dps[k][0])]
         for k in range(1, 8):
-            put(Us.at[k], Ur.at[k], uS.at[k], uR.at[k], dps[k])
+            put(Us.at[k], Ur.at[k], uS.at[0], uR.at[0], dps[k], False)
 
     def side():
         for b in range(3):
             dacc[:, blk(b)] += lax.dot_general(Ar[slot[b]].T, up_act[blk(b)], TB, preferred_element_type=f32)
 
     def owned(recv, ss, rs, to):
-        for k in range(1, 8):
-            got(recv.at[k], ss.at[k], rs.at[k])
+        got(recv.at[pl.ds(1, 7)], ss.at[0], rs.at[0])
         picks = [wanted(rem(dp - k + 8, 8)) for k in range(8)]
         for a in range(4):
             v = None
@@ -296,9 +289,6 @@
                 v = t if v is None else v + t
             to[a] = v.astype(bf16)
 
-    loc[0].wait()
-    for k in range(8):
-        (Br if k == 0 else Bs)[k] = b_ref[sels[k]]
     pl.semaphore_wait(bar, len(peers))
     def first(d, i):
         put(w_hbm.at[:, pl.ds(256 * i, 256)], Wp.at[wbase + i], w1S.at[d, i], w1R.at[d, i], (XP, XM)[d])
@@ -311,8 +301,16 @@
     gput(0, gsl(0, 0), ZP)
     gput(1, gsl(0, 0), ZM)
     gy(0)
+    live = lives[dp]
+    rows = lax.broadcasted_iota(jnp.int32, (384, 1), 0)
+    own = [ids[3 * dp + b] // 4 for b in range(3)]
+    slot = [rem(dp - own[b] + 8, 8) for b in range(3)]
+    sels = [wanted(dps[k][0])[1] for k in range(8)]
+    loc[0].wait()
+    for k in range(8):
+        (Br if k == 0 else Bs)[k] = b_ref[sels[k]]
     for k in range(1, 8):
-        put(Bs.at[k], Br.at[k], bS.at[k], bR.at[k], dps[k])
+        put(Bs.at[k], Br.at[k], bS.at[0], bR.at[0], dps[k], False)
     for cp in loc[5:]:
         cp.wait()
     wput(6, 0, 0, 4, SIB)
@@ -342,7 +340,7 @@
     came(0, 0); wput(4, 3, 0, 1, XP); came(0, 1); wput(5, 3, 1, 1, XP); wput(7, 3, 0, 2, SIB)
     came(1, 2); wput(13, 1, 2, 1, XM); came(1, 3); wput(14, 1, 3, 1, XM); wput(9, 1, 2, 2, SIB)
     for k in range(1, 8):
-        put(As.at[k], Ar.at[k], aS.at[k], aR.at[k], dps[k])
+        put(As.at[k], Ar.at[k], aS.at[0], aR.at[0], dps[k], False)
     both(0, 3)
     up_scatter()
     wgot(7, 3, 0, 2, 1); wgot(9, 1, 2, 2, 1)
@@ -368,6 +366,16 @@
     both(2, 1)
     backs(r2)
     both(2, 2)
+    for cp in sends:
+        cp.wait_send()
+    sends.clear()
+    left(Bs.at[pl.ds(1, 7)], bS.at[0])
+    left(part.at[1, pl.ds(0, 168)], p1S.at[1])
+    left(fold_r.at[1, pl.ds(1, 3)], p2S.at[1])
+    left(part.at[1, pl.ds(0, 168)], p3S.at[1])
+    left(Gg.at[pl.ds(0, 16)], gyS.at[0])
+    left(Zs.at[0], zS.at[0])
+    left(Zs.at[1], zS.at[1])
     wgot(4, 2, 0, 1); wput(11, 2, 0, 1, SIB)
     wgot(13, 2, 2, 1); wput(12, 2, 2, 1, SIB)
     both(2, 3)
@@ -377,8 +385,8 @@
     wgot(11, 2, 0, 1, 1); wgot(12, 2, 2, 1, 1); wgot(15, 2, 1, 1, 1); wgot(16, 2, 3, 1, 1)
     both(3, 0)
     pre(3, 1)
-    for j in range(8):
-        gl(j)
+    gl()
+    left(Gg.at[pl.ds(0, 8)], gfS.at[0])
     backs(r3)
     level(3, 1)
     pre(3, 2)
@@ -389,6 +397,7 @@
     backs(r4, 0, 2)
     level(3, 3)
     fold_y(0)
+    left(As.at[pl.ds(1, 7)], aS.at[0])
     pre(3, 4)
     backs(r4, 2, 2)
     level(3, 4)
@@ -396,7 +405,10 @@
     side()
     columns = lax.broadcasted_iota(jnp.int32, (1, 384), 1)
     dh[...] = jnp.where(columns < live, dacc[...], 0.0).astype(bf16)
+    outs = [pltpu.make_async_copy(s, d, oS.at[i]) for i, (s, d) in enumerate(((out, out_h), (dh, dh_h), (dg, dg_h), (ug, ug_h)))]
+    outs[1].start()
     owned(Tr, tS, tR, dg)
+    outs[2].start()
     for b in range(3):
         acc[0, 0, blk(b)] = jnp.dot(down_act[blk(b)], Br[slot[b]], preferred_element_type=f32)
     for h in (0, 1):
@@ -408,28 +420,30 @@
             t = t + Yr[j, h].astype(f32)
         out[r] = jnp.where(rows[192 * h:192 * h + 192] < live, t, 0.0).astype(bf16)
 
+    outs[0].start()
     owned(Ur, uS, uR, ug)
+    outs[3].start()
     for cp in sends:
         cp.wait_send()
-
-    def zw(i, _):
-        for h in (0, 1):
-            zcopy(i // 7, rem(i, 7), h, ZP).wait_send()
-        return 0
-    lax.fori_loop(0, 28, zw, 0)
+    left(Us.at[pl.ds(1, 7)], uS.at[0])
+    left(Ts.at[pl.ds(1, 7)], tS.at[0])
+    left(part.at[0, pl.ds(0, 168)], p1S.at[0])
+    left(fold_r.at[0, pl.ds(1, 3)], p2S.at[0])
+    left(part.at[0, pl.ds(0, 168)], p3S.at[0])
+    left(Zs.at[2], zS.at[2])
+    left(Zs.at[3], zS.at[3])
     for r in range(4):
         @pl.when(y != row(r, z))
         def _():
             for h in (0, 1):
                 ycopy(r, h).wait_send()
-
-
-def finish(a, b, c, d, oa, ob, oc, od, sems):
-    cps = [pltpu.make_async_copy(i, o, sems.at[k]) for k, (i, o) in enumerate(((a, oa), (b, ob), (c, oc), (d, od)))]
-    for cp in cps:
-        cp.start()
-    for cp in cps:
+    for cp in outs:
         cp.wait()
+
+
+def finish(a, b, c, d, oa, ob, oc, od):
+    for i, o in ((a, oa), (b, ob), (c, oc), (d, od)):
+        o[...] = i[...]
 
 
 def shards(hidden, down_weight, adapter_down, adapter_up, output_grad, adapter_per_block, live_rows):
@@ -444,8 +458,9 @@
             jax.ShapeDtypeStruct((384, 256), bf16), jax.ShapeDtypeStruct((832, 384), bf16),
             jax.ShapeDtypeStruct((4, 64, 832), bf16), jax.ShapeDtypeStruct((4, 64, 256), bf16)),
         in_specs=[S, S, A, A, A, A, A],
-        out_specs=(V, V, V, V),
+        out_specs=(A, A, A, A),
         scratch_shapes=[
+            M((384, 256), bf16), M((832, 384), bf16), M((4, 64, 832), bf16), M((4, 64, 256), bf16), D((4,)),
             M((832, 384), bf16), M((384, 832), bf16), M((384, 256), bf16), M((384, 256), bf16),
             M((4, 64, 832), bf16), M((4, 64, 256), bf16),
             M((32, 832, 256), bf16),
@@ -462,10 +477,10 @@
             M((3, 64, 832), bf16), M((3, 64, 256), bf16),
             M((2, 192, 128), f32), M((2, 8, 24, 128), f32), M((2, 24, 128), f32), M((2, 4, 24, 128), f32), M((2, 192, 128), f32),
             M((384, 64), bf16), M((384, 64), bf16),
-            D((9,)), D((17,)), D((17,)), D((2, 4)), D((2, 4)), D((8,)), D((8,)), D((8, 2)), D((8, 2)), D((8, 2)), D((8, 2)),
-            D((4, 7, 2)), D((4, 7, 2)), D((4, 2)), D((3, 2)),
-            D((8,)), D((8,)), D((8,)), D((8,)), D((8,)), D((8,)), D((8,)), D((8,)),
-            D((2, 8)), D((2, 8)), D((2, 4)), D((2, 4)), D((2, 8)), D((2, 8)),
+            D((9,)), D((17,)), D((17,)), D((2, 4)), D((2, 4)), D((8,)), D((8,)), D((1,)), D((8, 2)), D((1,)), D((1,)),
+            D((4,)), D((4, 7, 2)), D((4, 2)), D((3, 2)),
+            D((1,)), D((1,)), D((1,)), D((1,)), D((1,)), D((1,)), D((1,)), D((1,)),
+            D((2,)), D((2,)), D((2,)), D((2,)), D((2,)), D((2,)),
         ],
         name="layer",
         cost_estimate=pl.CostEstimate(flops=2 * 2 * 384 * 832 * 8192, bytes_accessed=6 * 2 ** 20, transcendentals=0),
@@ -475,7 +490,7 @@
     out, dh_t, dg_t, ug = pl.pallas_call(
         finish,
         out_shape=tuple(jax.ShapeDtypeStruct(v.shape, v.dtype) for v in parts),
-        in_specs=[A] * 4, out_specs=(A,) * 4, scratch_shapes=[D((4,))], name="finish",
+        in_specs=[V] * 4, out_specs=(V,) * 4, name="finish",
         cost_estimate=pl.CostEstimate(flops=0, bytes_accessed=4 * 2 ** 20, transcendentals=0),
     )(*parts)
     return out, dh_t.T, jnp.swapaxes(dg_t, 1, 2), ug

time: 163 us -> 118 us (0.72)
  Pallas kernels: 163 us -> 117 us
    pallas_call x1, Pallas kernels: 44.3 us -> 2.43 us  [shards(): pl.pallas_call(finish, out_shape=tuple((jax.ShapeDtypeStruct(v.shape, v.d...]
    pallas_call x1, Pallas kernels: 118 us -> 115 us  [shards(): pl.pallas_call(kernel, out_shape=(jax.ShapeDtypeStruct((384, 256), bf16),...]
where the time goes in v4:
time: 118 us
  Pallas kernels  117 us (99%)
    pallas_call x1, Pallas kernels, shards(): pl.pallas_call(kernel, out_shape=(jax.ShapeDtypeStruct((384, 256), bf16),...  115 us
    pallas_call x1, Pallas kernels, shards(): pl.pallas_call(finish, out_shape=tuple((jax.ShapeDtypeStruct(v.shape, v.d...  2.43 us

profile of v4, /device:TPU:1, one launch (start us, length us, event | category | flops | bytes accessed | tf_op | source)
XLA Modules:
  0.0 117.6 jit_solution(14974506677831412465)
XLA Ops:
  0.6 114.6 %layer.1 = (bf16[384,256]{1,0:T(8,128)(2,1)}, bf16[832,384]{1,0:T(8,128)(2,1)}, bf16[4,64,832]{2,1,0:T(8,128)(2,1)}, bf16[4,64,256]{2,1,0:T(8,128)(2,1)}) custom-call(s32[24]{0:T(128)} %ids.1, s32[8]{0:T(128)} %lives.1, bf16[832,384]{1,0:T(8,128)(2,1)} %bitcast.4, bf16[832,1024]{1,0:T(8,128)(2,1)} %w_hbm.1, bf16[4,64,832]{2,1,0:T(8,128)(2,1)} %bitcast.6, ...), custom_call_target="tpu_custom_call" | custom-call | flops 10468982784 | bytes 6291456 | tf_op jit(solution)/shard_map/layer/pallas_call | solution.py:455
  115.2 2.4 %finish.1 = (bf16[384,256]{1,0:T(8,128)(2,1)}, bf16[832,384]{1,0:T(8,128)(2,1)}, bf16[4,64,832]{2,1,0:T(8,128)(2,1)}, bf16[4,64,256]{2,1,0:T(8,128)(2,1)}) custom-call(bf16[384,256]{1,0:T(8,128)(2,1)} %get-tuple-element.12.a, bf16[832,384]{1,0:T(8,128)(2,1)} %get-tuple-element.13.b, bf16[4,64,832]{2,1,0:T(8,128)(2,1)} %get-tuple-element.14.c, ...), custom_call_target="tpu_custom_call" | custom-call | bytes 4194304 | tf_op jit(solution)/shard_map/finish/pallas_call | solution.py:490

commit v5 on v4

--- a/solution.py
+++ b/solution.py
@@ -399,9 +399,9 @@
     fold_y(0)
     left(As.at[pl.ds(1, 7)], aS.at[0])
     pre(3, 4)
-    backs(r4, 2, 2)
     level(3, 4)
     down_terms()
+    backs(r4, 2, 2)
     side()
     columns = lax.broadcasted_iota(jnp.int32, (1, 384), 1)
     dh[...] = jnp.where(columns < live, dacc[...], 0.0).astype(bf16)
@@ -441,9 +441,17 @@
         cp.wait()
 
 
-def finish(a, b, c, d, oa, ob, oc, od):
-    for i, o in ((a, oa), (b, ob), (c, oc), (d, od)):
-        o[...] = i[...]
+def finish(*refs):
+    ins, to, held, sems = refs[:4], refs[4:8], refs[8:12], refs[12]
+    come = [pltpu.make_async_copy(ins[k], held[k], sems.at[0, k]) for k in range(4)]
+    go = [pltpu.make_async_copy(held[k], to[k], sems.at[1, k]) for k in range(4)]
+    for cp in come:
+        cp.start()
+    for k in range(4):
+        come[k].wait()
+        go[k].start()
+    for cp in go:
+        cp.wait()
 
 
 def shards(hidden, down_weight, adapter_down, adapter_up, output_grad, adapter_per_block, live_rows):
@@ -490,7 +498,8 @@
     out, dh_t, dg_t, ug = pl.pallas_call(
         finish,
         out_shape=tuple(jax.ShapeDtypeStruct(v.shape, v.dtype) for v in parts),
-        in_specs=[V] * 4, out_specs=(V,) * 4, name="finish",
+        in_specs=[A] * 4, out_specs=(A,) * 4,
+        scratch_shapes=[M(v.shape, v.dtype) for v in parts] + [D((2, 4))], name="finish",
         cost_estimate=pl.CostEstimate(flops=0, bytes_accessed=4 * 2 ** 20, transcendentals=0),
     )(*parts)
     return out, dh_t.T, jnp.swapaxes(dg_t, 1, 2), ug

time: 118 us -> 118 us (level)
  no operation moved by 1% of the time
where the time goes in v5:
time: 118 us
  Pallas kernels  117 us (99%)
    pallas_call x1, Pallas kernels, shards(): pl.pallas_call(kernel, out_shape=(jax.ShapeDtypeStruct((384, 256), bf16),...  115 us

profile of v5, /device:TPU:1, one launch (start us, length us, event | category | flops | bytes accessed | tf_op | source)
XLA Modules:
  0.0 117.7 jit_solution(2825352969958679550)
XLA Ops:
  0.6 114.6 %layer.1 = (bf16[384,256]{1,0:T(8,128)(2,1)}, bf16[832,384]{1,0:T(8,128)(2,1)}, bf16[4,64,832]{2,1,0:T(8,128)(2,1)}, bf16[4,64,256]{2,1,0:T(8,128)(2,1)}) custom-call(s32[24]{0:T(128)} %ids.1, s32[8]{0:T(128)} %lives.1, bf16[832,384]{1,0:T(8,128)(2,1)} %bitcast.4, bf16[832,1024]{1,0:T(8,128)(2,1)} %w_hbm.1, bf16[4,64,832]{2,1,0:T(8,128)(2,1)} %bitcast.6, ...), custom_call_target="tpu_custom_call" | custom-call | flops 10468982784 | bytes 6291456 | tf_op jit(solution)/shard_map/layer/pallas_call | solution.py:463
  115.2 2.3 %finish.1 = (bf16[384,256]{1,0:T(8,128)(2,1)}, bf16[832,384]{1,0:T(8,128)(2,1)}, bf16[4,64,832]{2,1,0:T(8,128)(2,1)}, bf16[4,64,256]{2,1,0:T(8,128)(2,1)}) custom-call(bf16[384,256]{1,0:T(8,128)(2,1)} %get-tuple-element.12.refs_0_, bf16[832,384]{1,0:T(8,128)(2,1)} %get-tuple-element.13.refs_1_, bf16[4,64,832]{2,1,0:T(8,128)(2,1)} %get-tuple-element.14.refs_2_, ...), custom_call_target="tpu_custom_call" | custom-call | bytes 4194304 | tf_op jit(solution)/shard_map/finish/pallas_call | solution.py:498
